TPU v7x, 32 devices: a whole 2x2x4 slice. The times are simulated.
32 devices in a mesh: tok: 8 (over y, x, core), head: 4 (over z).
Axes of the slice: x: 2, y: 2, z: 4, core: 2. Of those that a mesh axis runs over, the one named last changes fastest.
Arguments:
- patches: bfloat16 [8192, 768], P(('tok', 'head')), may hold values from -6 to 6
- classes: bfloat16 [2400, 768], P(('tok', 'head')), may hold values from -6 to 6
- slot_lengths: int32 [8, 2], P('tok'), may hold values from 64 to 960, as said below
- w_qkv: bfloat16 [768, 2304], P(('tok', 'head')), may hold values from -0.21875 to 0.21875
- w_out: bfloat16 [768, 768], P(('tok', 'head')), may hold values from -4 to 4
- w_up: bfloat16 [768, 3072], P(('tok', 'head')), may hold values from -0.21875 to 0.21875
- w_down: bfloat16 [3072, 768], P(('tok', 'head')), may hold values from -0.109375 to 0.109375
- w_patch: bfloat16 [768, 768], P(('tok', 'head')), may hold values from -0.21875 to 0.21875
- w_class: bfloat16 [768, 768], P(('tok', 'head')), may hold values from -0.21875 to 0.21875
- norm1: bfloat16 [768], P(('tok', 'head')), may hold values from 0.099609375 to 1.8984375
- norm2: bfloat16 [768], P(('tok', 'head')), may hold values from 0.099609375 to 1.8984375
- mask_gain: float32 [150], replicated, may hold values from 0.1 to 1.9
- d_masks: float32 [8192, 150], P(('tok', 'head')), may hold values from -6 to 6
Outputs:
- masks: float32 [8192, 150], P(('tok', 'head'))
- grad_patches: float32 [8192, 768], P(('tok', 'head'))
- grad_classes: float32 [2400, 768], P(('tok', 'head'))
- grad_qkv: float32 [768, 2304], P(('tok', 'head'))
- grad_out: float32 [768, 768], P(('tok', 'head'))
- grad_up: float32 [768, 3072], P(('tok', 'head'))
- grad_down: float32 [3072, 768], P(('tok', 'head'))
- grad_patch_proj: float32 [768, 768], P(('tok', 'head'))
- grad_class_proj: float32 [768, 768], P(('tok', 'head'))
- grad_norm1: float32 [768], P(('tok', 'head'))
- grad_norm2: float32 [768], P(('tok', 'head'))
- grad_mask_gain: float32 [150], replicated
Inputs may be any that keep to these rules, and one draw needn't show every extreme that they name: `slot_lengths`: each slot holds two images, one of 64 to 255 patches and one of more than 768 patches, in either order, together at most 1024; in some slot they fill it exactly.
All inputs are finite; a program needn't handle non-finite values.
Results may differ from a plain program's by a relative error of at most 0.022.
Values may be sent and summed in bfloat16 or wider, within the bound.
A program may use at most 128 MiB of HBM per device.

v0:
```python
import jax
import jax.numpy as jnp
from jax import lax
from jax.sharding import PartitionSpec as P

HEADS = 12
NCLS = 150


def layer_norm(values, gain):
    centre = values - jnp.mean(values, axis=-1, keepdims=True)
    spread = jnp.mean(centre * centre, axis=-1, keepdims=True)
    return centre * lax.rsqrt(spread + 1e-05) * gain


def unit_rows(values):
    return values * lax.rsqrt(jnp.sum(values * values, axis=-1, keepdims=True) + 1e-06)


def exact_gelu(values):
    return jax.nn.gelu(values, approximate=False)


def dot_plain(left, right):
    return jnp.dot(left, right, preferred_element_type=jnp.float32)


def dot_left_t(left, right):
    return lax.dot_general(
        left, right, (((0,), (0,)), ((), ())), preferred_element_type=jnp.float32
    )


def dot_right_t(left, right):
    return lax.dot_general(
        left, right, (((1,), (1,)), ((), ())), preferred_element_type=jnp.float32
    )


def flat_rows(matrix):
    return matrix.reshape(-1, 128)


def per_device(
    patches,
    classes,
    slot_lengths,
    w_qkv,
    w_out,
    w_up,
    w_down,
    w_patch,
    w_class,
    norm1,
    norm2,
    mask_gain,
    d_masks,
):
    tok_rows = patches.shape[0]
    cls_rows = classes.shape[0]
    all_rows = tok_rows + cls_rows
    width = patches.shape[1]
    groups = lax.axis_size("head")
    my_group = lax.axis_index("head")
    local_heads = HEADS // groups
    head_size = width // HEADS
    lead_len = slot_lengths[0, 0]
    tail_len = slot_lengths[0, 1]

    def segment_of(source, offset):
        place = source * tok_rows + offset
        patch_seg = jnp.where(place < lead_len, 0, jnp.where(place < lead_len + tail_len, 1, -1))
        class_seg = (source * cls_rows + offset - tok_rows) // NCLS
        return jnp.where(offset < tok_rows, patch_seg, class_seg)

    tok_seg = segment_of(my_group, jnp.arange(tok_rows))
    spread_rows = jnp.arange(groups * all_rows)
    head_seg = segment_of(spread_rows // all_rows, spread_rows % all_rows)
    allowed = (head_seg[:, None] == head_seg[None, :]) & (head_seg[None, :] >= 0)
    shards = (w_qkv, w_out, w_up, w_down, w_patch, w_class, norm1, norm2)
    gathered = (
        lax.all_gather(shards[0], ("tok", "head"), axis=0, tiled=True),
        lax.all_gather(shards[1], ("tok", "head"), axis=0, tiled=True),
        lax.all_gather(shards[2], ("tok", "head"), axis=0, tiled=True),
        lax.all_gather(shards[3], ("tok", "head"), axis=0, tiled=True),
        lax.all_gather(shards[4], ("tok", "head"), axis=0, tiled=True),
        lax.all_gather(shards[5], ("tok", "head"), axis=0, tiled=True),
        lax.all_gather(shards[6], ("tok", "head"), axis=0, tiled=True),
        lax.all_gather(shards[7], ("tok", "head"), axis=0, tiled=True),
    )
    full_qkv, full_out, full_up, full_down, full_patch, full_class, gain_one, gain_two = gathered
    stacked = jnp.concatenate([patches, classes], axis=0).astype(jnp.float32)
    first_in = layer_norm(stacked, gain_one.astype(jnp.float32)).astype(jnp.bfloat16)
    qkv_rows = (
        dot_plain(first_in, full_qkv)
        .astype(jnp.bfloat16)
        .reshape(all_rows, 3, groups, local_heads * head_size)
    )
    moved = lax.all_to_all(qkv_rows, "head", split_axis=2, concat_axis=0, tiled=True)
    moved = moved.reshape(groups * all_rows, 3, local_heads, head_size)
    queries = jnp.transpose(moved[:, 0], (1, 0, 2))
    key_rows = jnp.transpose(moved[:, 1], (1, 0, 2))
    value_rows = jnp.transpose(moved[:, 2], (1, 0, 2))

    def attend(parts):
        query, key_part, value_part = parts
        scores = jnp.where(allowed, dot_right_t(query, key_part) * 0.125, -1e30)
        top_score = jnp.max(scores, axis=1, keepdims=True)
        expo = jnp.exp(scores - top_score)
        total = jnp.sum(expo, axis=1, keepdims=True)
        probs = (expo / total).astype(jnp.bfloat16)
        result = dot_plain(probs, value_part).astype(jnp.bfloat16)
        return (result, top_score[:, 0] + jnp.log(total[:, 0]))

    head_out, log_total = lax.map(attend, (queries, key_rows, value_rows))
    sending = jnp.transpose(head_out, (1, 0, 2)).reshape(
        groups * all_rows, 1, local_heads * head_size
    )
    attended = lax.all_to_all(sending, "head", split_axis=0, concat_axis=1, tiled=True).reshape(
        all_rows, width
    )
    hidden = stacked + dot_plain(attended, full_out)
    second_in = layer_norm(hidden, gain_two.astype(jnp.float32)).astype(jnp.bfloat16)
    up_rows = dot_plain(second_in, full_up)
    gelu_rows = exact_gelu(up_rows).astype(jnp.bfloat16)
    after = (hidden + dot_plain(gelu_rows, full_down)).astype(jnp.bfloat16)
    patch_proj = dot_plain(after[:tok_rows], full_patch)
    class_proj = dot_plain(after[tok_rows:], full_class)
    patch_unit = unit_rows(patch_proj).astype(jnp.bfloat16)
    class_unit = unit_rows(class_proj).astype(jnp.bfloat16)
    slot_classes = lax.all_gather(class_unit, "head", axis=0, tiled=True)
    raw_both = dot_right_t(patch_unit, slot_classes)
    first_image = tok_seg[:, None] == 0
    raw = jnp.where(first_image, raw_both[:, :NCLS], raw_both[:, NCLS:])
    centre = raw - jnp.mean(raw, axis=1, keepdims=True)
    inv_sigma = lax.rsqrt(jnp.mean(centre * centre, axis=1, keepdims=True) + 1e-05)
    normed = centre * inv_sigma
    valid = (tok_seg >= 0).astype(jnp.float32)[:, None]
    masks = normed * mask_gain * valid
    regathered = (
        lax.all_gather(shards[0], ("tok", "head"), axis=0, tiled=True),
        lax.all_gather(shards[1], ("tok", "head"), axis=0, tiled=True),
        lax.all_gather(shards[2], ("tok", "head"), axis=0, tiled=True),
        lax.all_gather(shards[3], ("tok", "head"), axis=0, tiled=True),
        lax.all_gather(shards[4], ("tok", "head"), axis=0, tiled=True),
        lax.all_gather(shards[5], ("tok", "head"), axis=0, tiled=True),
        lax.all_gather(shards[6], ("tok", "head"), axis=0, tiled=True),
        lax.all_gather(shards[7], ("tok", "head"), axis=0, tiled=True),
    )
    back_qkv, back_out, back_up, back_down, back_patch, back_class, back_one, back_two = regathered
    mask_cot = d_masks * valid
    grad_mask = lax.psum(jnp.sum(mask_cot * normed, axis=0), ("tok", "head"))
    scaled = mask_cot * mask_gain
    d_raw = inv_sigma * (
        scaled
        - jnp.mean(scaled, axis=1, keepdims=True)
        - normed * jnp.mean(scaled * normed, axis=1, keepdims=True)
    )
    zero_part = jnp.zeros_like(d_raw)
    d_raw_both = jnp.concatenate(
        [jnp.where(first_image, d_raw, zero_part), jnp.where(first_image, zero_part, d_raw)], axis=1
    ).astype(jnp.bfloat16)
    d_patch_unit = dot_plain(d_raw_both, slot_classes)
    d_slot_classes = dot_left_t(d_raw_both, patch_unit)
    d_class_unit = lax.psum_scatter(
        d_slot_classes.astype(jnp.bfloat16), "head", scatter_dimension=0, tiled=True
    ).astype(jnp.float32)
    _, patch_pull = jax.vjp(unit_rows, patch_proj)
    d_patch_proj = patch_pull(d_patch_unit)[0].astype(jnp.bfloat16)
    _, class_pull = jax.vjp(unit_rows, class_proj)
    d_class_proj = class_pull(d_class_unit)[0].astype(jnp.bfloat16)
    grad_patch_w = dot_left_t(after[:tok_rows], d_patch_proj)
    grad_class_w = dot_left_t(after[tok_rows:], d_class_proj)
    d_after = jnp.concatenate(
        [dot_right_t(d_patch_proj, back_patch), dot_right_t(d_class_proj, back_class)], axis=0
    )
    d_after_low = d_after.astype(jnp.bfloat16)
    grad_down_w = dot_left_t(gelu_rows, d_after_low)
    d_gelu = dot_right_t(d_after_low, back_down)
    _, gelu_pull = jax.vjp(exact_gelu, up_rows)
    d_up_rows = gelu_pull(d_gelu)[0].astype(jnp.bfloat16)
    grad_up_w = dot_left_t(second_in, d_up_rows)
    d_second_in = dot_right_t(d_up_rows, back_up)
    _, norm_two_pull = jax.vjp(layer_norm, hidden, back_two.astype(jnp.float32))
    d_hidden_norm, grad_gain_two = norm_two_pull(d_second_in)
    d_hidden = d_after + d_hidden_norm
    d_hidden_low = d_hidden.astype(jnp.bfloat16)
    grad_out_w = dot_left_t(attended, d_hidden_low)
    d_attended = (
        dot_right_t(d_hidden_low, back_out)
        .astype(jnp.bfloat16)
        .reshape(all_rows, groups, local_heads * head_size)
    )
    d_head_out = lax.all_to_all(d_attended, "head", split_axis=1, concat_axis=0, tiled=True)
    d_head_out = jnp.transpose(
        d_head_out.reshape(groups * all_rows, local_heads, head_size), (1, 0, 2)
    )

    def attend_back(parts):
        query, key_part, value_part, log_row, d_result = parts
        scores = jnp.where(allowed, dot_right_t(query, key_part) * 0.125, -1e30)
        probs = jnp.exp(scores - log_row[:, None])
        d_probs = dot_right_t(d_result, value_part)
        inner = jnp.sum(probs * d_probs, axis=1, keepdims=True)
        d_scores = jnp.where(allowed, probs * (d_probs - inner), 0.0).astype(jnp.bfloat16)
        d_query = (dot_plain(d_scores, key_part) * 0.125).astype(jnp.bfloat16)
        d_key = (dot_left_t(d_scores, query) * 0.125).astype(jnp.bfloat16)
        d_value = dot_left_t(probs.astype(jnp.bfloat16), d_result).astype(jnp.bfloat16)
        return jnp.stack([d_query, d_key, d_value], axis=0)

    d_moved = lax.map(attend_back, (queries, key_rows, value_rows, log_total, d_head_out))
    d_moved = jnp.transpose(d_moved, (2, 1, 0, 3)).reshape(
        groups * all_rows, 3, 1, local_heads * head_size
    )
    d_qkv = lax.all_to_all(d_moved, "head", split_axis=0, concat_axis=2, tiled=True).reshape(
        all_rows, 3 * width
    )
    grad_qkv_w = dot_left_t(first_in, d_qkv)
    d_first_in = dot_right_t(d_qkv, back_qkv)
    _, norm_one_pull = jax.vjp(layer_norm, stacked, back_one.astype(jnp.float32))
    d_stacked_norm, grad_gain_one = norm_one_pull(d_first_in)
    d_stacked = d_hidden + d_stacked_norm
    every_sum = (
        lax.psum_scatter(flat_rows(grad_qkv_w), ("tok", "head"), scatter_dimension=0, tiled=True),
        lax.psum_scatter(flat_rows(grad_out_w), ("tok", "head"), scatter_dimension=0, tiled=True),
        lax.psum_scatter(flat_rows(grad_up_w), ("tok", "head"), scatter_dimension=0, tiled=True),
        lax.psum_scatter(flat_rows(grad_down_w), ("tok", "head"), scatter_dimension=0, tiled=True),
        lax.psum_scatter(flat_rows(grad_patch_w), ("tok", "head"), scatter_dimension=0, tiled=True),
        lax.psum_scatter(flat_rows(grad_class_w), ("tok", "head"), scatter_dimension=0, tiled=True),
        lax.psum_scatter(grad_gain_one, ("tok", "head"), scatter_dimension=0, tiled=True),
        lax.psum_scatter(grad_gain_two, ("tok", "head"), scatter_dimension=0, tiled=True),
    )
    sum_qkv, sum_out, sum_up, sum_down, sum_patch, sum_class, sum_one, sum_two = every_sum
    sum_qkv = sum_qkv.reshape(-1, 3 * width)
    sum_out = sum_out.reshape(-1, width)
    sum_up = sum_up.reshape(-1, grad_up_w.shape[1])
    sum_down = sum_down.reshape(-1, width)
    sum_patch = sum_patch.reshape(-1, width)
    sum_class = sum_class.reshape(-1, width)
    return (
        masks,
        d_stacked[:tok_rows],
        d_stacked[tok_rows:],
        sum_qkv,
        sum_out,
        sum_up,
        sum_down,
        sum_patch,
        sum_class,
        sum_one,
        sum_two,
        grad_mask,
    )


def solution(mesh):
    placed = (
        P(("tok", "head"), None),
        P(("tok", "head"), None),
        P("tok", None),
        P(("tok", "head"), None),
        P(("tok", "head"), None),
        P(("tok", "head"), None),
        P(("tok", "head"), None),
        P(("tok", "head"), None),
        P(("tok", "head"), None),
        P(("tok", "head")),
        P(("tok", "head")),
        P(),
        P(("tok", "head"), None),
    )
    return jax.shard_map(
        per_device,
        mesh=mesh,
        in_specs=placed,
        out_specs=(
            P(("tok", "head"), None),
            P(("tok", "head"), None),
            P(("tok", "head"), None),
            P(("tok", "head"), None),
            P(("tok", "head"), None),
            P(("tok", "head"), None),
            P(("tok", "head"), None),
            P(("tok", "head"), None),
            P(("tok", "head"), None),
            P(("tok", "head")),
            P(("tok", "head")),
            P(),
        ),
        check_vma=False,
    )
```

profile of v0, /device:TPU:0, one launch (start us, length us, event | category | flops | bytes accessed | tf_op | source)
XLA Modules:
  0.0 1142.7 jit_solution(17414211933732478703)
XLA Ops:
  11.7 42.1 %all-reduce.7 = (bf16[768]{0:T(1024)(128)(2,1)S(1)}, bf16[768]{0:T(1024)(128)(2,1)}) all-reduce(bf16[768]{0:T(1024)(128)(2,1)S(1)} %dynamic-update-slice, bf16[768]{0:T(1024)(128)(2,1)S(1)} %dynamic-update-slice.1), channel_id=1, replica_groups=mesh['tok'=8,'head'=4] {'tok','head'}, use_global_device_ids=true, to_apply=%add | all-reduce | flops 1536 | bytes 6144
  56.9 16.8 %all-gather.8.cloned.1.call-done = bf16[768,2304]{1,0:T(8,128)(2,1)} async-done(((bf16[24,2304]{1,0:T(8,128)(2,1)}), bf16[768,2304]{1,0:T(8,128)(2,1)}) %all-gather.8.cloned.1.call-update) | async-done | bytes 3538960 | tf_op jit(solution)/shard_map/all_gather | solution.py:82
  87.4 39.5 %all-to-all-done = bf16[331,3,4,192]{0,3,1,2:T(8,128)(2,1)S(1)} async-done(((bf16[331,3,4,192]{0,3,1,2:T(8,128)(2,1)}), bf16[331,3,4,192]{0,3,1,2:T(8,128)(2,1)S(1)}, u32[]{:S(2)}, u32[]{:S(2)}) %all-to-all-start) | async-done | bytes 1525280 | tf_op jit(solution)/shard_map/all_to_all | solution.py:99
  135.4 20.0 %while.24 = (s32[]{:T(128)}, bf16[3,1324,64]{1,2,0:T(8,128)(2,1)}, f32[3,1324]{1,0:T(4,128)}, bf16[3,1324,64]{2,1,0:T(8,128)(2,1)S(1)}, bf16[3,1324,64]{2,1,0:T(...) while((s32[]{:T(128)}, bf16[3,1324,64]{1,2,0:T(8,128)(2,1)}, ...), condition=%wide.region_5.6_spmd.clone, body=%wide.region_2.5_spmd.clone.sunk | while | flops 466375008 | bytes 26860552 | solution.py:115
  171.7 13.3 %all-to-all-done.1 = bf16[4,2,31776]{2,1,0:T(2,128)(2,1)} async-done(((bf16[4,2,31776]{2,1,0:T(2,128)(2,1)}), bf16[4,2,31776]{2,1,0:T(2,128)(2,1)}, u32[]{:S(2)}, u32[]{:S(2)}) %all-to-all-start.1) | async-done | bytes 508448 | tf_op jit(solution)/shard_map/all_to_all | solution.py:119
  185.0 4.8 reshape.345
  189.8 4.5 copy.97
  200.7 15.8 %all-gather.12.cloned.1.call-done = bf16[768,3072]{1,0:T(8,128)(2,1)} async-done(((bf16[24,3072]{1,0:T(8,128)(2,1)}), bf16[768,3072]{1,0:T(8,128)(2,1)}) %all-gather.12.cloned.1.call-update) | async-done | bytes 4718608 | tf_op jit(solution)/shard_map/all_gather | solution.py:84
  216.5 13.7 %multiply_convert_fusion = (bf16[331,3072]{1,0:T(8,128)(2,1)S(1)}, f32[331,3072]{1,0:T(8,128)}, f32[331,3072]{1,0:T(8,128)}) fusion(bf16[768,3072]{1,0:T(8,128)(2,1)} %all-gather.12.cloned.1.call-done, f32[331,768]{1,0:T(8,128)S(1)} %get-tuple-element.287, f32[768]{0:T(1024)S(1)} %convert_element_type.89, f32[331]{0:T(512)S(1)} %fusion.105, ...), kind=kOutput, calls=%fused_computation.63 | convolution fusion | flops 1628964864 | bytes 15909464 | tf_op jit(solution)/shard_map/dot_general | solution.py:25
  230.3 51.3 %all-gather.14.cloned.1.call-done = bf16[3072,768]{1,0:T(8,128)(2,1)} async-done(((bf16[96,768]{1,0:T(8,128)(2,1)}), bf16[3072,768]{1,0:T(8,128)(2,1)}) %all-gather.14.cloned.1.call-update) | async-done | bytes 4718608 | tf_op jit(solution)/shard_map/all_gather | solution.py:85
  281.6 4.9 fusion.65
  286.5 50.7 %all-gather.18.cloned.1.call-done = bf16[768,768]{1,0:T(8,128)(2,1)} async-done(((bf16[24,768]{1,0:T(8,128)(2,1)}), bf16[768,768]{1,0:T(8,128)(2,1)}) %all-gather.18.cloned.1.call-update) | async-done | bytes 1179664 | tf_op jit(solution)/shard_map/all_gather | solution.py:87
  339.7 15.7 %all-gather = bf16[4,75,768]{2,1,0:T(8,128)(2,1)S(1)} all-gather(bf16[1,75,768]{2,1,0:T(8,128)(2,1)S(1)} %fusion.83), channel_id=1, replica_groups=mesh['tok'=8,'head'=4] {'head'}, dimensions={0}, use_global_device_ids=true | all-gather | bytes 576000 | tf_op jit(solution)/shard_map/all_gather | solution.py:131
  355.6 37.3 %all-gather.16.cloned.1.call-done = bf16[768,768]{1,0:T(8,128)(2,1)} async-done(((bf16[24,768]{1,0:T(8,128)(2,1)}), bf16[768,768]{1,0:T(8,128)(2,1)}) %all-gather.16.cloned.1.call-update) | async-done | bytes 1179664 | tf_op jit(solution)/shard_map/all_gather | solution.py:86
  397.8 18.4 %fusion.4 = bf16[80,768]{1,0:T(8,128)(2,1)S(1)} fusion(bf16[300,768]{1,0:T(8,128)(2,1)S(1)} %convolution_convert_fusion.2), kind=kCustom, calls=%all-reduce-scatter | all-reduce-scatter fusion | flops 245761 | bytes 584192
  427.6 7.8 add_convert_fusion
  451.8 10.6 all-to-all-done.2
  464.4 36.8 %while.25 = (s32[]{:T(128)}, bf16[3,3,1324,64]{2,3,0,1:T(8,128)(2,1)}, bf16[3,1324,64]{2,1,0:T(8,128)(2,1)S(1)}, bf16[3,1324,64]{2,1,0:T(8,128)(2,1)S(1)}, f32[3...) while((s32[]{:T(128)}, ...), condition=%wide.region_21.22_spmd.clone, body=%wide.region_19.21_spmd.clone.sunk | while | flops 1148393856 | bytes 57665852 | solution.py:211
  501.2 4.6 copy.106
  505.8 64.0 %all_to_all.60 = bf16[1324,3,1,192]{3,1,2,0:T(4,128)(2,1)} all-to-all(bf16[1324,3,1,192]{3,1,2,0:T(4,128)(2,1)S(1)} %copy.106), channel_id=1, replica_groups=mesh['tok'=8,'head'=4] {'head'}, dimensions={0} | all-to-all | bytes 3050496 | tf_op jit(solution)/shard_map/all_to_all | solution.py:215
  569.9 5.6 copy.109
  577.0 5.1 fusion.111
  582.2 7.9 reshape.324
  591.3 6.8 fusion.115
  598.1 10.9 reshape.328
  610.3 7.9 fusion.90
  618.2 10.7 reshape.330
  636.9 38.2 %all-reduce.6 = (f32[768]{0:T(1024)S(1)}, f32[768]{0:T(1024)S(1)}, f32[150]{0:T(256)}) all-reduce(f32[768]{0:T(1024)S(1)} %get-tuple-element.224, f32[768]{0:T(1024)S(1)} %copy-done.53, f32[150]{0:T(256)S(1)} %copy-done.52), channel_id=9, replica_groups=mesh['tok'=8,'head'=4] {'tok','head'}, use_global_device_ids=true, to_apply=%region_31.32.clone | all-reduce | flops 1686 | bytes 13488
  679.3 47.9 %reduce-scatter.19.cloned.1.call-done = f32[144,128]{1,0:T(8,128)} async-done(((f32[4608,128]{1,0:T(8,128)}), f32[144,128]{1,0:T(8,128)}) %reduce-scatter.19.cloned.1.call-update) | async-done | bytes 73744 | tf_op jit(solution)/shard_map/reduce_scatter | solution.py:229
  728.8 123.1 %reduce-scatter.9.cloned.1.call-done = f32[432,128]{1,0:T(8,128)} async-done(((f32[13824,128]{1,0:T(8,128)}), f32[432,128]{1,0:T(8,128)}) %reduce-scatter.9.cloned.1.call-update) | async-done | bytes 221200 | tf_op jit(solution)/shard_map/reduce_scatter | solution.py:224
  853.5 139.1 %reduce-scatter.13.cloned.1.call-done = f32[576,128]{1,0:T(8,128)} async-done(((f32[18432,128]{1,0:T(8,128)}), f32[576,128]{1,0:T(8,128)}) %reduce-scatter.13.cloned.1.call-update) | async-done | bytes 294928 | tf_op jit(solution)/shard_map/reduce_scatter | solution.py:226
  994.4 139.5 %reduce-scatter.15.cloned.1.call-done = f32[576,128]{1,0:T(8,128)} async-done(((f32[18432,128]{1,0:T(8,128)}), f32[576,128]{1,0:T(8,128)}) %reduce-scatter.15.cloned.1.call-update) | async-done | bytes 294928 | tf_op jit(solution)/shard_map/reduce_scatter | solution.py:227
  (302 shorter events, 166.4 us)
Async XLA Ops:
  7.2 66.6 %all-gather.8.cloned.1.call-start = ((), (), s32[]{:S(2)}) async-start(), calls=%async_computation.10 | async-start | bytes 3649536 | tf_op jit(solution)/shard_map/all_gather | solution.py:82
  7.9 190.2 %all-gather.10.cloned.1.call-start = ((), (), s32[]{:S(2)}) async-start(), calls=%async_computation.11 | async-start | bytes 1216512 | tf_op jit(solution)/shard_map/all_gather | solution.py:83
  8.7 207.9 %all-gather.12.cloned.1.call-start = ((), (), s32[]{:S(2)}) async-start(), calls=%async_computation.12 | async-start | bytes 4866048 | tf_op jit(solution)/shard_map/all_gather | solution.py:84
  9.4 272.2 %all-gather.14.cloned.1.call-start = ((), (), s32[]{:S(2)}) async-start(), calls=%async_computation.13 | async-start | bytes 4866048 | tf_op jit(solution)/shard_map/all_gather | solution.py:85
  53.8 20.0 %copy-start.32 = (f32[768]{0:T(1024)}, f32[768]{0:T(1024)S(1)}, u32[]{:S(2)}) copy-start(f32[768]{0:T(1024)S(1)} %convert_element_type.86) | copy-start | bytes 9220
  55.0 18.8 %copy-start.34 = (f32[331]{0:T(512)}, f32[331]{0:T(512)S(1)}, u32[]{:S(2)}) copy-start(f32[331]{0:T(512)S(1)} %broadcast_multiply_fusion.1) | copy-start | bytes 3976
  56.9 16.9 %copy-start.39 = (f32[331]{0:T(512)}, f32[331]{0:T(512)S(1)}, u32[]{:S(2)}) copy-start(f32[331]{0:T(512)S(1)} %fusion.104) | copy-start | bytes 3976
  79.9 46.9 %all-to-all-start = ((bf16[331,3,4,192]{0,3,1,2:T(8,128)(2,1)}), bf16[331,3,4,192]{0,3,1,2:T(8,128)(2,1)S(1)}, u32[]{:S(2)}, u32[]{:S(2)}) async-start(bf16[331,3,4,192]{0,3,1,2:T(8,128)(2,1)} %copy.91), calls=%async_computation | async-start | bytes 3538944 | tf_op jit(solution)/shard_map/all_to_all | solution.py:99
  83.5 253.7 %all-gather.18.cloned.1.call-start = ((), (), s32[]{:S(2)}) async-start(), calls=%async_computation.15 | async-start | bytes 1216512 | tf_op jit(solution)/shard_map/all_gather | solution.py:87
  155.3 38.9 %copy-start.8 = (bf16[3,1324,64]{2,1,0:T(8,128)(2,1)}, bf16[3,1324,64]{2,1,0:T(8,128)(2,1)S(1)}, u32[]{:S(2)}) copy-start(bf16[3,1324,64]{2,1,0:T(8,128)(2,1)S(1)} %get-tuple-element.497) | copy-start | bytes 1525252
  155.3 38.9 %copy-start.10 = (bf16[3,1324,64]{2,1,0:T(8,128)(2,1)}, bf16[3,1324,64]{2,1,0:T(8,128)(2,1)S(1)}, u32[]{:S(2)}) copy-start(bf16[3,1324,64]{2,1,0:T(8,128)(2,1)S(1)} %get-tuple-element.498) | copy-start | bytes 1525252
  160.8 37.4 %copy-start.2 = (bf16[256,768]{1,0:T(8,128)(2,1)S(1)}, bf16[256,768]{1,0:T(8,128)(2,1)}, u32[]{:S(2)}) copy-start(bf16[256,768]{1,0:T(8,128)(2,1)} %param.17) | copy-start | bytes 1179652
  160.8 37.4 %copy-start.19 = (bf16[75,768]{1,0:T(8,128)(2,1)S(1)}, bf16[75,768]{1,0:T(8,128)(2,1)}, u32[]{:S(2)}) copy-start(bf16[75,768]{1,0:T(8,128)(2,1)} %param.18) | copy-start | bytes 345604
  163.8 21.3 %all-to-all-start.1 = ((bf16[4,2,31776]{2,1,0:T(2,128)(2,1)}), bf16[4,2,31776]{2,1,0:T(2,128)(2,1)}, u32[]{:S(2)}, u32[]{:S(2)}) async-start(bf16[4,2,31776]{2,1,0:T(2,128)(2,1)} %reshape.344), calls=%async_computation.1 | async-start | bytes 1019904 | tf_op jit(solution)/shard_map/all_to_all | solution.py:119
  167.9 225.0 %all-gather.16.cloned.1.call-start = ((), (), s32[]{:S(2)}) async-start(), calls=%async_computation.14 | async-start | bytes 1216512 | tf_op jit(solution)/shard_map/all_gather | solution.py:86
  168.5 507.8 %reduce-scatter.17.cloned.1.call-start = ((), (), s32[]{:S(2)}) async-start(), calls=%async_computation.20 | async-start | bytes 2433024 | tf_op jit(solution)/shard_map/reduce_scatter | solution.py:228
  200.4 237.5 %copy-start.4 = (f32[331,768]{1,0:T(8,128)}, f32[331,768]{1,0:T(8,128)S(1)}, u32[]{:S(2)}) copy-start(f32[331,768]{1,0:T(8,128)S(1)} %get-tuple-element.287) | copy-start | bytes 3050500
  200.4 29.9 %copy-start.36 = (f32[331]{0:T(512)}, f32[331]{0:T(512)S(1)}, u32[]{:S(2)}) copy-start(f32[331]{0:T(512)S(1)} %broadcast_multiply_fusion) | copy-start | bytes 3976
  200.6 29.6 %copy-start.46 = (f32[331]{0:T(512)}, f32[331]{0:T(512)S(1)}, u32[]{:S(2)}) copy-start(f32[331]{0:T(512)S(1)} %multiply_reduce_fusion.3) | copy-start | bytes 3976
  200.7 29.6 %copy-start.41 = (f32[331]{0:T(512)}, f32[331]{0:T(512)S(1)}, u32[]{:S(2)}) copy-start(f32[331]{0:T(512)S(1)} %fusion.105) | copy-start | bytes 3976
  230.2 56.2 %copy-start.21 = (bf16[331,3072]{1,0:T(8,128)(2,1)}, bf16[331,3072]{1,0:T(8,128)(2,1)S(1)}, u32[]{:S(2)}) copy-start(bf16[331,3072]{1,0:T(8,128)(2,1)S(1)} %get-tuple-element.272) | copy-start | bytes 6100996
  286.5 108.9 %copy-start.27 = (f32[256,150]{0,1:T(8,128)S(1)}, f32[256,150]{0,1:T(8,128)}, u32[]{:S(2)}) copy-start(f32[256,150]{0,1:T(8,128)} %param.29) | copy-start | bytes 460804
  286.5 108.9 %copy-start.51 = (f32[150]{0:T(256)S(1)}, f32[150]{0:T(256)}, u32[]{:S(2)}) copy-start(f32[150]{0:T(256)} %param.28) | copy-start | bytes 1804
  339.0 16.7 %copy-start.58 = (f32[75]{0:T(128)}, f32[75]{0:T(128)S(1)}, u32[]{:S(2)}) copy-start(f32[75]{0:T(128)S(1)} %get-tuple-element.289) | copy-start | bytes 904
  339.0 56.4 %copy-start.48 = (f32[75]{0:T(128)}, f32[75]{0:T(128)S(1)}, u32[]{:S(2)}) copy-start(f32[75]{0:T(128)S(1)} %add_rsqrt_fusion.2) | copy-start | bytes 904
  416.3 8.0 collective-permute-start
  422.1 255.7 %reduce-scatter.11.cloned.1.call-start = ((), (), s32[]{:S(2)}) async-start(), calls=%async_computation.17 | async-start | bytes 2433024 | tf_op jit(solution)/shard_map/reduce_scatter | solution.py:225
  444.3 18.1 %all-to-all-start.2 = ((bf16[331,4,192]{0,2,1:T(8,128)(2,1)}), bf16[331,4,192]{0,2,1:T(8,128)(2,1)}, u32[]{:S(2)}, u32[]{:S(2)}) async-start(bf16[331,4,192]{0,2,1:T(8,128)(2,1)} %bitcast.18), calls=%async_computation.2 | async-start | bytes 1179648 | tf_op jit(solution)/shard_map/all_to_all | solution.py:194
  448.5 278.8 %reduce-scatter.19.cloned.1.call-start = ((), (), s32[]{:S(2)}) async-start(), calls=%async_computation.21 | async-start | bytes 2433024 | tf_op jit(solution)/shard_map/reduce_scatter | solution.py:229
  451.6 400.3 %reduce-scatter.9.cloned.1.call-start = ((), (), s32[]{:S(2)}) async-start(), calls=%async_computation.16 | async-start | bytes 7299072 | tf_op jit(solution)/shard_map/reduce_scatter | solution.py:224
  590.1 402.5 %reduce-scatter.13.cloned.1.call-start = ((), (), s32[]{:S(2)}) async-start(), calls=%async_computation.18 | async-start | bytes 9732096 | tf_op jit(solution)/shard_map/reduce_scatter | solution.py:226
  609.1 524.8 %reduce-scatter.15.cloned.1.call-start = ((), (), s32[]{:S(2)}) async-start(), calls=%async_computation.19 | async-start | bytes 9732096 | tf_op jit(solution)/shard_map/reduce_scatter | solution.py:227
  (51 other events, 240.7 us)
Sparse Core Ops, SparseCore 0:
  10.8 62.9 all-gather.7
  76.6 73.9 all-gather.9
  153.3 63.1 all-gather.11
  219.2 62.3 all-gather.13
  284.2 52.8 all-gather.17
  339.8 53.0 all-gather.15
  422.2 97.4 reduce-scatter.16
  525.9 97.9 reduce-scatter.10
  629.2 98.0 reduce-scatter.18
  733.7 118.1 reduce-scatter.8
  857.8 134.8 reduce-scatter.12
  999.4 134.4 reduce-scatter.14
where the time goes:
time: 1150 us; the launch traced here: 1140 us
  waiting for transfers between devices  688 us (60%)
  blocking collectives  178 us (15%)
  local copies, waits for them, and re-layouts  110 us (10%)
  matrix products  108 us (9%)
  other arithmetic  25.1 us (2%)
  between operations  17.4 us (2%)
  starting transfers between devices  15.7 us (1%)
    reduce_scatter x1, waiting for transfers between devices, per_device(): lax.psum_scatter(flat_rows(grad_down_w), ('tok', 'head'), scatter_dimensi...  139 us
    reduce_scatter x1, waiting for transfers between devices, per_device(): lax.psum_scatter(flat_rows(grad_up_w), ('tok', 'head'), scatter_dimension...  139 us
    reduce_scatter x1, waiting for transfers between devices, per_device(): lax.psum_scatter(flat_rows(grad_qkv_w), ('tok', 'head'), scatter_dimensio...  123 us
    unnamed x3, blocking collectives  98.7 us
    all_to_all x1, blocking collectives, per_device(): lax.all_to_all(d_moved, 'head', split_axis=0, concat_axis=2, tiled=True)  64 us
    all_gather x1, waiting for transfers between devices, per_device(): lax.all_gather(shards[3], ('tok', 'head'), axis=0, tiled=True)  51.3 us
    all_gather x1, waiting for transfers between devices, per_device(): lax.all_gather(shards[5], ('tok', 'head'), axis=0, tiled=True)  50.7 us
    reduce_scatter x1, waiting for transfers between devices, per_device(): lax.psum_scatter(flat_rows(grad_class_w), ('tok', 'head'), scatter_dimens...  47.9 us
  transfers between devices with their start and end apart: 16, of which 12 were waited for; matrix products, arithmetic and copies ran while one was open for 20% of the time, Pallas kernels for 0%

commit v1 on v0

--- a/solution.py
+++ b/solution.py
@@ -1,6 +1,8 @@
 import jax
 import jax.numpy as jnp
 from jax import lax
+from jax.experimental import pallas as pl
+from jax.experimental.pallas import tpu as pltpu
 from jax.sharding import PartitionSpec as P
 
 HEADS = 12
@@ -253,6 +255,999 @@
     )
 
 
+ROWS = 336
+SLOT_ROWS = 4 * ROWS
+PATCH = 256
+CLS = 80
+REAL = 75
+PIECE = 80
+LEAD = 16
+MESH = pl.DeviceIdType.MESH
+BF = jnp.bfloat16
+F32 = jnp.float32
+
+
+def position():
+    tok = lax.axis_index("tok")
+    return lax.div(tok, 4), lax.rem(lax.div(tok, 2), 2), lax.rem(tok, 2), lax.axis_index("head")
+
+
+def device(y, x, c, z):
+    return {"tok": y * 4 + x * 2 + c, "head": z}
+
+
+def enter(y, x, c, z):
+    barrier = pltpu.get_barrier_semaphore()
+    others = [device(1 - y, x, c, z)]
+    for turn in range(1, 16):
+        flip_x, flip_c, step = turn // 8, (turn // 4) % 2, turn % 4
+        others.append(
+            device(
+                y,
+                1 - x if flip_x else x,
+                1 - c if flip_c else c,
+                lax.rem(z + step, 4),
+            )
+        )
+    for other in others:
+        pl.semaphore_signal(barrier, inc=1, device_id=other, device_id_type=MESH)
+    pl.semaphore_wait(barrier, len(others))
+
+
+class Net:
+    def __init__(self, send_sem, recv_sem, here):
+        self.send_sem, self.recv_sem, self.here = send_sem, recv_sem, here
+        self.sends, self.recvs, self.open = 0, 0, []
+
+    def land(self, count=1):
+        first = self.recvs
+        self.recvs += count
+        return first
+
+    def send(self, src, dst, to, slot, skip=None):
+        index = self.sends
+        self.sends += 1
+        copy = pltpu.make_async_remote_copy(
+            src_ref=src,
+            dst_ref=dst,
+            send_sem=self.send_sem.at[index],
+            recv_sem=self.recv_sem.at[slot],
+            device_id=to,
+            device_id_type=MESH,
+        )
+        if skip is None:
+            copy.start()
+            self.open.append((copy, None))
+        else:
+            pl.when(jnp.logical_not(skip))(copy.start)
+            self.open.append((copy, skip))
+
+            @pl.when(skip)
+            def _():
+                pltpu.make_async_copy(src, dst, self.recv_sem.at[slot]).start()
+
+    def local(self, src, dst, slot):
+        pltpu.make_async_copy(src, dst, self.recv_sem.at[slot]).start()
+
+    def wait(self, ref, slot):
+        pltpu.make_async_copy(ref, ref, self.recv_sem.at[slot]).wait()
+
+    def finish(self):
+        for copy, skip in self.open:
+            if skip is None:
+                copy.wait_send()
+            else:
+                pl.when(jnp.logical_not(skip))(copy.wait_send)
+        self.open = []
+
+
+def rows_of(start, size):
+    return pl.ds(pl.multiple_of(start, 16), size)
+
+
+def lanes_of(start, size):
+    return pl.ds(pl.multiple_of(start, 128), size)
+
+
+def gather_kernel(
+    xin, dmx, aux, wqa, wra, wd, xs, dmh, auxh, wq, wr, wdn, stq, str_, bq, br, send_sem, recv_sem
+):
+    y, x, c, z = position()
+    tok = y * 4 + x * 2 + c
+    quarter = 2 * x + c
+    enter(y, x, c, z)
+    net = Net(send_sem, recv_sem, None)
+    sib, xdev, ydev = device(y, x, 1 - c, z), device(y, 1 - x, c, z), device(1 - y, x, c, z)
+    half = wra.shape[1] // 2
+    h1, h2 = pl.ds(0, half), pl.ds(half, half)
+    d1, d2 = pl.ds(0, 384), pl.ds(384, 384)
+
+    home = 2 * c + x
+    got_lead, got_piece, got_dm, got_aux = net.land(4), net.land(4), net.land(), net.land()
+    for q in range(4):
+        to = device(y, q // 2, q % 2, home)
+        mine = (z == home) & (quarter == q)
+        off = LEAD + PIECE * q
+        net.send(
+            xin.at[pl.ds(off, PIECE)],
+            xs.at[rows_of(z * ROWS + off, PIECE)],
+            to,
+            got_piece + z,
+            mine,
+        )
+        net.send(
+            xin.at[pl.ds(0, LEAD)], xs.at[rows_of(z * ROWS, LEAD)], to, got_lead + z, mine
+        )
+    to = device(y, lax.div(z, 2), lax.rem(z, 2), home)
+    mine = (z == home) & (quarter == z)
+    net.send(aux, auxh, to, got_aux, mine)
+
+    got_q, got_r, got_d = net.land(4), net.land(4), net.land(4)
+    net.local(wqa, stq.at[z], got_q + z)
+    net.local(wra, str_.at[z], got_r + z)
+    own_d = wdn.at[rows_of((tok * 4 + z) * 96, 96)]
+    net.local(wd, own_d, got_d + z)
+    peers = [device(y, x, c, lax.rem(z + step, 4)) for step in (1, 3, 2)]
+    for peer in peers:
+        net.send(wqa, stq.at[z], peer, got_q + z)
+    for peer in peers:
+        net.send(wra, str_.at[z], peer, got_r + z)
+    for peer in peers:
+        net.send(wd, own_d, peer, got_d + z)
+    net.send(dmx, dmh, to, got_dm, mine)
+
+    def piece(source, owner):
+        return xs.at[rows_of(source * ROWS + LEAD + PIECE * owner, PIECE)]
+
+    fwd_s, fwd_x, fwd_xs = net.land(4), net.land(4), net.land(4)
+    for src in range(4):
+        net.wait(piece(src, quarter), got_piece + src)
+        net.send(piece(src, quarter), piece(src, quarter), xdev, fwd_x + src)
+        net.send(piece(src, quarter), piece(src, quarter), sib, fwd_s + src)
+
+    def blk(t):
+        return rows_of(t * 96, 96)
+
+    def big(t):
+        return rows_of(t * 384, 384)
+
+    for src in range(4):
+        net.wait(stq.at[src], got_q + src)
+
+    def join(stage, block, width):
+        def body(i, carry):
+            cols = lanes_of(i * width, width)
+            parts = [stage[src, :, cols].astype(F32) for src in range(4)]
+            block[:, cols] = jnp.concatenate(parts, axis=0).astype(BF)
+            return carry
+
+        lax.fori_loop(0, block.shape[1] // width, body, 0)
+
+    join(stq, bq, 384)
+    t_x, t_y = tok + 2 - 4 * x, tok + 4 - 8 * y
+    t_xy = t_x + 4 - 8 * y
+    own_half, other_half = lanes_of(1152 * x, 1152), lanes_of(1152 * (1 - x), 1152)
+    q_own, q_x, q_y, q_xy, q_s = net.land(), net.land(), net.land(), net.land(), net.land(4)
+    net.send(bq.at[:, other_half], wq.at[blk(tok)], xdev, q_x)
+    net.send(bq.at[:, own_half], wq.at[blk(tok)], ydev, q_y)
+    net.local(bq.at[:, own_half], wq.at[blk(tok)], q_own)
+    net.send(bq.at[:, own_half], wq.at[blk(tok)], sib, q_s)
+
+    other = quarter + 2 - 4 * x
+    for src in range(4):
+        net.wait(piece(src, other), fwd_x + src)
+        net.send(piece(src, other), piece(src, other), sib, fwd_xs + src)
+    net.wait(wq.at[blk(t_x)], q_x)
+    net.send(wq.at[blk(t_x)], wq.at[blk(t_x)], ydev, q_xy)
+    net.send(wq.at[blk(t_x)], wq.at[blk(t_x)], sib, q_s + 1)
+
+    for src in range(4):
+        net.wait(str_.at[src], got_r + src)
+    join(str_, br, 384)
+    r_own = net.land(2)
+    r_x, r_y, r_s = net.land(4), net.land(4), net.land(8)
+    e_x, e_y, e_s = net.land(4), net.land(4), net.land(8)
+    net.send(br.at[:, h1], wr.at[blk(tok), h1], xdev, r_x)
+    net.send(br.at[:, h2], wr.at[blk(tok), h2], ydev, r_y)
+    for src in range(4):
+        net.wait(wdn.at[rows_of((tok * 4 + src) * 96, 96)], got_d + src)
+    net.send(wdn.at[big(tok), d1], wdn.at[big(tok), d1], xdev, e_x)
+    net.send(wdn.at[big(tok), d2], wdn.at[big(tok), d2], ydev, e_y)
+    net.send(br.at[:, h1], wr.at[blk(tok), h1], ydev, r_y + 1)
+    net.send(br.at[:, h2], wr.at[blk(tok), h2], xdev, r_x + 1)
+    net.send(wdn.at[big(tok), d1], wdn.at[big(tok), d1], ydev, e_y + 1)
+    net.send(wdn.at[big(tok), d2], wdn.at[big(tok), d2], xdev, e_x + 1)
+    net.local(br.at[:, h1], wr.at[blk(tok), h1], r_own)
+    net.local(br.at[:, h2], wr.at[blk(tok), h2], r_own + 1)
+    net.send(br.at[:, h1], wr.at[blk(tok), h1], sib, r_s)
+    net.send(br.at[:, h2], wr.at[blk(tok), h2], sib, r_s + 1)
+    net.send(wdn.at[big(tok), d1], wdn.at[big(tok), d1], sib, e_s)
+    net.send(wdn.at[big(tok), d2], wdn.at[big(tok), d2], sib, e_s + 1)
+
+    net.wait(wq.at[blk(t_y)], q_y)
+    net.send(wq.at[blk(t_y)], wq.at[blk(t_y)], sib, q_s + 2)
+    net.wait(wq.at[blk(t_xy)], q_xy)
+    net.send(wq.at[blk(t_xy)], wq.at[blk(t_xy)], sib, q_s + 3)
+
+    def passed(ref, rows, cols, slot, onward):
+        net.wait(ref.at[rows, cols], slot)
+        for to_dev, index in onward:
+            net.send(ref.at[rows, cols], ref.at[rows, cols], to_dev, index)
+
+    passed(wr, blk(t_x), h1, r_x, [(ydev, r_y + 2), (sib, r_s + 2)])
+    passed(wr, blk(t_y), h2, r_y, [(xdev, r_x + 2), (sib, r_s + 3)])
+    passed(wdn, big(t_x), d1, e_x, [(ydev, e_y + 2), (sib, e_s + 2)])
+    passed(wdn, big(t_y), d2, e_y, [(xdev, e_x + 2), (sib, e_s + 3)])
+    passed(wr, blk(t_y), h1, r_y + 1, [(sib, r_s + 4)])
+    passed(wr, blk(t_x), h2, r_x + 1, [(sib, r_s + 5)])
+    passed(wdn, big(t_y), d1, e_y + 1, [(sib, e_s + 4)])
+    passed(wdn, big(t_x), d2, e_x + 1, [(sib, e_s + 5)])
+    passed(wr, blk(t_xy), h1, r_y + 2, [(sib, r_s + 6)])
+    passed(wr, blk(t_xy), h2, r_x + 2, [(sib, r_s + 7)])
+    passed(wdn, big(t_xy), d1, e_y + 2, [(sib, e_s + 6)])
+    passed(wdn, big(t_xy), d2, e_x + 2, [(sib, e_s + 7)])
+
+    flip = 1 - 2 * c
+    for i, t in enumerate((tok, t_x, t_y, t_xy)):
+        net.wait(wq.at[blk(t + flip)], q_s + i)
+    order = ((tok, 0), (tok, 1), (t_x, 0), (t_y, 1), (t_y, 0), (t_x, 1), (t_xy, 0), (t_xy, 1))
+    for i, (t, second) in enumerate(order):
+        net.wait(wr.at[blk(t + flip), h2 if second else h1], r_s + i)
+        net.wait(wdn.at[big(t + flip), d2 if second else d1], e_s + i)
+    net.wait(wq.at[blk(tok)], q_own)
+    net.wait(wr.at[blk(tok), h1], r_own)
+    net.wait(wr.at[blk(tok), h2], r_own + 1)
+    sibling = quarter + flip
+    for src in range(4):
+        net.wait(xs.at[rows_of(src * ROWS, LEAD)], got_lead + src)
+        net.wait(piece(src, sibling), fwd_s + src)
+        net.wait(piece(src, sibling + 2 - 4 * x), fwd_xs + src)
+    net.wait(dmh, got_dm)
+    net.wait(auxh, got_aux)
+    net.finish()
+
+
+def nn(left, right):
+    return jnp.dot(left, right, preferred_element_type=F32)
+
+
+def nt(left, right):
+    return lax.dot_general(left, right, (((1,), (1,)), ((), ())), preferred_element_type=F32)
+
+
+def tn(left, right):
+    return lax.dot_general(left, right, (((0,), (0,)), ((), ())), preferred_element_type=F32)
+
+
+def segments(row, lead_len, tail_len):
+    source = (
+        (row >= ROWS).astype(jnp.int32)
+        + (row >= 2 * ROWS).astype(jnp.int32)
+        + (row >= 3 * ROWS).astype(jnp.int32)
+    )
+    offset = row - source * ROWS
+    patch = source * PATCH + offset
+    patch_seg = jnp.where(patch < lead_len, 0, jnp.where(patch < lead_len + tail_len, 1, -1))
+    number = offset - PATCH
+    class_seg = jnp.where(source >= 2, 1, 0)
+    filler = number >= REAL
+    seg = jnp.where(offset < PATCH, patch_seg, jnp.where(filler, -1, class_seg))
+    return seg, filler
+
+
+def normalise(values):
+    centre = values - jnp.mean(values, axis=-1, keepdims=True)
+    scale = lax.rsqrt(jnp.mean(centre * centre, axis=-1, keepdims=True) + 1e-05)
+    return centre * scale, scale
+
+
+def own_lanes(c, head, shape):
+    lane = lax.broadcasted_iota(jnp.int32, shape, len(shape) - 1)
+    group = lane // 64 - c
+    if head is None:
+        return (group >= 0) & (group < 3)
+    return group == head
+
+
+BLOCK = 192
+
+
+def forward_kernel(xs, wq, aux, wp, zn, qr, kr, vr, out, stats, kh, vh):
+    c = lax.rem(lax.axis_index("tok"), 2)
+    lead_len, tail_len = aux[0:1, 0:1], aux[1:2, 0:1]
+    keep = own_lanes(c, None, (768, 256))
+    for part in range(3):
+        cols = lanes_of(384 * part + 128 * c, 256)
+        wp[:, 256 * part : 256 * part + 256] = jnp.where(keep, wq[:, cols], 0.0).astype(BF)
+
+    def project(i, carry):
+        rows = rows_of(i * ROWS, ROWS)
+        normed = normalise(xs[rows, :].astype(F32))[0].astype(BF)
+        zn[rows, :] = normed
+        qr[rows, :] = (nn(normed, wp[:, 0:256]).astype(BF) * 0.125).astype(BF)
+        kr[rows, :] = nn(normed, wp[:, 256:512]).astype(BF)
+        vr[rows, :] = nn(normed, wp[:, 512:768]).astype(BF)
+        return carry
+
+    lax.fori_loop(0, 4, project, 0)
+    for head in range(3):
+        mine = own_lanes(c, head, (SLOT_ROWS, 256))
+        kh[head] = jnp.where(mine, kr[...], 0.0).astype(BF)
+        vh[head] = jnp.where(mine, vr[...], 0.0).astype(BF)
+    key_row = lax.broadcasted_iota(jnp.int32, (1, SLOT_ROWS), 1)
+    key_seg, key_filler = segments(key_row, lead_len, tail_len)
+    key_seg = jnp.where(key_seg < 0, -5, key_seg)
+    masked = jnp.where(key_filler, -3e38, -1e30)
+
+    def attend(i, carry):
+        rows = rows_of(i * BLOCK, BLOCK)
+        row = lax.broadcasted_iota(jnp.int32, (BLOCK, 1), 0) + i * BLOCK
+        seg = segments(row, lead_len, tail_len)[0]
+        query = qr[rows, :]
+        lane = lax.broadcasted_iota(jnp.int32, (BLOCK, 128), 1)
+        total_out = jnp.zeros((BLOCK, 256), F32)
+        kept = jnp.zeros((BLOCK, 128), F32)
+        for head in range(3):
+            scores = jnp.where(seg == key_seg, nt(query, kh[head]), masked)
+            top = jnp.max(scores, axis=1, keepdims=True)
+            expo = jnp.exp(scores - top)
+            total = jnp.sum(expo, axis=1, keepdims=True)
+            probs = (expo * (1.0 / total)).astype(BF)
+            total_out = total_out + nn(probs, vh[head])
+            kept = jnp.where(lane == head, top + jnp.log(total), kept)
+        out[rows, :] = total_out.astype(BF)
+        stats[rows, :] = kept
+        return carry
+
+    lax.fori_loop(0, SLOT_ROWS // BLOCK, attend, 0)
+
+
+def backward_kernel(
+    zn, qr, kr, vr, out, stats, d_out, wp, aux, gq, d_first, stat_t, delta, dq, dqkv, znt
+):
+    c = lax.rem(lax.axis_index("tok"), 2)
+    lead_len, tail_len = aux[0:1, 0:1], aux[1:2, 0:1]
+    stat_t[...] = stats[...].T
+    head_of = own_lanes(c, None, (8, 256))
+    lane = lax.broadcasted_iota(jnp.int32, (8, 256), 1)
+    row8 = lax.broadcasted_iota(jnp.int32, (8, 256), 0)
+    picker = jnp.where(head_of & (lane // 64 - c == row8), 1.0, 0.0)
+    product = d_out[...].astype(F32) * out[...].astype(F32)
+    delta[...] = lax.dot_general(
+        picker,
+        product,
+        (((1,), (1,)), ((), ())),
+        precision=lax.Precision.HIGHEST,
+        preferred_element_type=F32,
+    )
+    dq[...] = jnp.zeros_like(dq)
+    query_row = lax.broadcasted_iota(jnp.int32, (1, SLOT_ROWS), 1)
+    query_seg = segments(query_row, lead_len, tail_len)[0]
+
+    def step(j, carry):
+        rows = rows_of(j * BLOCK, BLOCK)
+        row = lax.broadcasted_iota(jnp.int32, (BLOCK, 1), 0) + j * BLOCK
+        seg, filler = segments(row, lead_len, tail_len)
+        seg = jnp.where(seg < 0, -5, seg)
+        masked = jnp.where(filler, -3e38, -1e30)
+        keys, values = kr[rows, :], vr[rows, :]
+        queries, d_results = qr[...], d_out[...]
+        allowed = seg == query_seg
+        d_key = jnp.zeros((BLOCK, 256), F32)
+        d_value = jnp.zeros((BLOCK, 256), F32)
+        for head in range(3):
+            mine = own_lanes(c, head, (BLOCK, 256))
+            key = jnp.where(mine, keys, 0.0).astype(BF)
+            value = jnp.where(mine, values, 0.0).astype(BF)
+            scores = jnp.where(allowed, nt(key, queries), masked)
+            probs = jnp.exp(scores - stat_t[head : head + 1, :])
+            d_probs = nt(value, d_results)
+            d_scores = jnp.where(
+                allowed, probs * (d_probs - delta[head : head + 1, :]), 0.0
+            ).astype(BF)
+            d_value = jnp.where(mine, nn(probs.astype(BF), d_results), d_value)
+            d_key = jnp.where(mine, nn(d_scores, queries), d_key)
+            dq[...] += tn(d_scores, key)
+        dqkv[rows, 256:512] = d_key.astype(BF)
+        dqkv[rows, 512:768] = d_value.astype(BF)
+        return carry
+
+    lax.fori_loop(0, SLOT_ROWS // BLOCK, step, 0)
+    dqkv[:, 0:256] = (dq[...] * 0.125).astype(BF)
+    znt[...] = zn[...].T
+
+    def first(i, carry):
+        rows = rows_of(i * ROWS, ROWS)
+        d_first[rows, :] = nt(dqkv[rows, :], wp[...]).astype(BF)
+        return carry
+
+    lax.fori_loop(0, 4, first, 0)
+
+    def weight(i, carry):
+        rows = rows_of(i * 256, 256)
+        gq[rows, :] = nn(znt[rows, :], dqkv[...]).astype(BF)
+        return carry
+
+    lax.fori_loop(0, 3, weight, 0)
+
+
+def group_of(y, x, c, z):
+    quarter = 2 * x + c
+    return [
+        (device(y, x, 1 - c, z), quarter + 1 - 2 * c),
+        (device(y, 1 - x, c, z), quarter + 2 - 4 * x),
+        (device(y, 1 - x, 1 - c, z), quarter + 3 - 4 * x - 2 * c),
+    ]
+
+
+TILE = 256
+
+
+def middle_kernel(
+    xs, o_mine, wr, wdn, dmh, aux, gain,
+    gr, gd, dh, d_out, masks, gain_part,
+    wr_v, wd_v, xb, obuf, att, znt, zn2, gl, slope, du, h_f, dz_f, dzb, pp_f, cn, dcn, dcbuf, dob,
+    inv, send_sem, recv_sem,
+):
+    y, x, c, z = position()
+    quarter = 2 * x + c
+    enter(y, x, c, z)
+    net = Net(send_sem, recv_sem, None)
+    group = group_of(y, x, c, z)
+    got_x, got_wr, got_wd = net.land(), net.land(), net.land()
+    got_o, got_cn, got_dc, got_do = net.land(4), net.land(4), net.land(4), net.land(4)
+    own_rows = rows_of(quarter * ROWS, ROWS)
+    for to, q in group:
+        net.send(o_mine.at[rows_of(q * ROWS, ROWS)], obuf.at[quarter], to, got_o + quarter)
+    net.local(o_mine.at[own_rows], obuf.at[quarter], got_o + quarter)
+    net.local(xs.at[own_rows], xb, got_x)
+    net.local(wr, wr_v, got_wr)
+    net.local(wdn, wd_v, got_wd)
+    lead_len, tail_len = aux[0:1, 0:1], aux[1:2, 0:1]
+    row = lax.broadcasted_iota(jnp.int32, (PATCH, 1), 0) + quarter * ROWS
+    seg = segments(row, lead_len, tail_len)[0]
+    first_image = seg == 0
+    valid = jnp.where(seg >= 0, 1.0, 0.0)
+    up, down = 3072, wd_v
+    w_out, w_patch, w_class = up, up + 768, up + 1536
+
+    net.wait(xb, got_x)
+    for q in range(4):
+        net.wait(obuf.at[q], got_o + q)
+    for side in range(2):
+        a, b = obuf[2 * side], obuf[2 * side + 1]
+        base = 384 * side
+        att[:, base : base + 128] = a[:, 0:128]
+        att[:, base + 128 : base + 256] = a[:, 128:256] + b[:, 0:128]
+        att[:, base + 256 : base + 384] = b[:, 128:256]
+    net.wait(wr_v, got_wr)
+    h_f[...] = xb[...].astype(F32) + nn(att[...], wr_v[:, w_out : w_out + 768])
+    normed, scale = normalise(h_f[...])
+    inv[...] = jnp.broadcast_to(scale, inv.shape)
+    zn2[...] = normed.astype(BF)
+    znt[...] = normed.T.astype(BF)
+
+    def up_step(i, carry):
+        cols = lanes_of(i * TILE, TILE)
+        u = nn(zn2[...], wr_v[:, cols])
+        cdf = 0.5 * (1.0 + lax.erf(u * 0.7071067811865476))
+        gl[:, cols] = (u * cdf).astype(BF)
+        slope[:, cols] = cdf + u * (jnp.exp(-0.5 * u * u) * 0.3989422804014327)
+        return carry
+
+    lax.fori_loop(0, up // TILE, up_step, 0)
+    net.wait(wd_v, got_wd)
+    z2 = (h_f[...] + nn(gl[...], wd_v[...])).astype(BF)
+    z2p, z2c = z2[0:PATCH], z2[PATCH:ROWS]
+
+    def unit(values):
+        return values * lax.rsqrt(jnp.sum(values * values, axis=-1, keepdims=True) + 1e-06)
+
+    def unit_back(values, cot):
+        r = lax.rsqrt(jnp.sum(values * values, axis=-1, keepdims=True) + 1e-06)
+        return r * cot - values * (r * r * r * jnp.sum(values * cot, axis=-1, keepdims=True))
+
+    cc = nn(z2c, wr_v[:, w_class : w_class + 768])
+    own_cls = rows_of(quarter * CLS, CLS)
+    cn[own_cls, :] = unit(cc).astype(BF)
+    for to, q in group:
+        net.send(cn.at[own_cls], cn.at[own_cls], to, got_cn + quarter)
+    pp = nn(z2p, wr_v[:, w_patch : w_patch + 768])
+    pp_f[...] = pp
+    pn = unit(pp).astype(BF)
+    for to, q in group:
+        net.wait(cn.at[rows_of(q * CLS, CLS)], got_cn + q)
+    low, high = cn[0 : 2 * CLS, :], cn[2 * CLS : 4 * CLS, :]
+    wide = 2 * CLS
+    lane = lax.broadcasted_iota(jnp.int32, (1, wide), 1)
+    real = jnp.where(lane >= CLS, lane - CLS, lane) < REAL
+    raw = jnp.where(first_image, nt(pn, low), nt(pn, high))
+
+    def mean(values):
+        return jnp.sum(jnp.where(real, values, 0.0), axis=1, keepdims=True) * (0.5 / REAL)
+
+    centre = jnp.where(real, raw - mean(raw), 0.0)
+    sigma = lax.rsqrt(mean(centre * centre) + 1e-05)
+    xhat = centre * sigma
+    mask_gain = gain[0:1, 0:wide]
+    masks[:, wide:256] = jnp.zeros((PATCH, 256 - wide), BF)
+    masks[:, 0:wide] = (xhat * mask_gain * valid).astype(BF)
+    dm = dmh[:, 0:wide].astype(F32) * valid
+    gain_part[...] = jnp.zeros_like(gain_part)
+    gain_part[0:1, 0:wide] = jnp.sum(dm * xhat, axis=0, keepdims=True)
+    dx = jnp.where(real, dm * mask_gain, 0.0)
+    d_raw = jnp.where(real, sigma * (dx - mean(dx) - xhat * mean(dx * xhat)), 0.0)
+    d_low = jnp.where(first_image, d_raw, 0.0).astype(BF)
+    d_high = jnp.where(first_image, 0.0, d_raw).astype(BF)
+    dcn[0:wide, :] = tn(d_low, pn).astype(BF)
+    dcn[wide : 2 * wide, :] = tn(d_high, pn).astype(BF)
+    for to, q in group:
+        net.send(dcn.at[rows_of(q * CLS, CLS)], dcbuf.at[quarter], to, got_dc + quarter)
+    net.local(dcn.at[own_cls], dcbuf.at[quarter], got_dc + quarter)
+    d_pn = nn(d_low, low) + nn(d_high, high)
+    d_pp = unit_back(pp_f[...], d_pn).astype(BF)
+    gr[:, w_patch : w_patch + 768] = tn(z2p, d_pp).astype(BF)
+    dz_f[0:PATCH, :] = nt(d_pp, wr_v[:, w_patch : w_patch + 768])
+    for q in range(4):
+        net.wait(dcbuf.at[q], got_dc + q)
+    d_cn = dcbuf[0].astype(F32) + dcbuf[1].astype(F32) + dcbuf[2].astype(F32) + dcbuf[3].astype(F32)
+    d_cc = unit_back(cc, d_cn).astype(BF)
+    gr[:, w_class : w_class + 768] = tn(z2c, d_cc).astype(BF)
+    dz_f[PATCH:ROWS, :] = nt(d_cc, wr_v[:, w_class : w_class + 768])
+    dzb[...] = dz_f[...].astype(BF)
+
+    def down_step(i, carry):
+        cols = lanes_of(i * TILE, TILE)
+        d_u = (nt(dzb[...], wd_v[cols, :]) * slope[:, cols]).astype(BF)
+        du[:, cols] = d_u
+        gd[cols, :] = tn(gl[:, cols], dzb[...]).astype(BF)
+        gr[:, cols] = nn(znt[...], d_u).astype(BF)
+        return carry
+
+    lax.fori_loop(0, up // TILE, down_step, 0)
+    d_zn = nt(du[...], wr_v[:, 0:up])
+    normed = h_f[...]
+    normed = (normed - jnp.mean(normed, axis=-1, keepdims=True)) * inv[:, 0:1]
+    d_h = dz_f[...] + inv[:, 0:1] * (
+        d_zn
+        - jnp.mean(d_zn, axis=-1, keepdims=True)
+        - normed * jnp.mean(d_zn * normed, axis=-1, keepdims=True)
+    )
+    dh[...] = d_h
+    d_hb = d_h.astype(BF)
+    dob[...] = nt(d_hb, wr_v[:, w_out : w_out + 768]).astype(BF)
+
+    def piece(q):
+        return dob.at[:, lanes_of(384 * lax.div(q, 2) + 128 * lax.rem(q, 2), 256)]
+
+    for to, q in group:
+        net.send(piece(q), d_out.at[own_rows], to, got_do + quarter)
+    net.local(piece(quarter), d_out.at[own_rows], got_do + quarter)
+    gr[:, w_out : w_out + 768] = tn(att[...], d_hb).astype(BF)
+    for q in range(4):
+        net.wait(d_out.at[rows_of(q * ROWS, ROWS)], got_do + q)
+    net.finish()
+
+
+def add_into(total, part, width):
+    def body(i, carry):
+        cols = lanes_of(i * width, width)
+        total[:, cols] = (total[:, cols].astype(F32) + part[:, cols].astype(F32)).astype(BF)
+        return carry
+
+    lax.fori_loop(0, total.shape[1] // width, body, 0)
+
+
+def split_rows(block, stage, width):
+    def body(i, carry):
+        cols = lanes_of(i * width, width)
+        values = block[:, cols].astype(F32)
+        for part in range(4):
+            stage[part, :, cols] = values[24 * part : 24 * part + 24].astype(BF)
+        return carry
+
+    lax.fori_loop(0, block.shape[1] // width, body, 0)
+
+
+def sum_parts(stage, total, width):
+    def body(i, carry):
+        cols = lanes_of(i * width, width)
+        total[:, cols] = (
+            stage[0, :, cols].astype(F32)
+            + stage[1, :, cols].astype(F32)
+            + stage[2, :, cols].astype(F32)
+            + stage[3, :, cols].astype(F32)
+        )
+        return carry
+
+    lax.fori_loop(0, total.shape[1] // width, body, 0)
+
+
+def reduce_kernel(
+    gr, gd, gq, d_first, dh, xs, masks, gain_part,
+    d_rows, mask_rows, sum_q, sum_r, sum_d, gain_sum,
+    xb, pr, pd, rr, rd, ry1, rx1, rx2, ry2, dy1, dx1, dx2, dy2, sp, rz, rzd,
+    pq, rq, hq, ryq, rxq, fq, spq, rzq, fa, fb, fc, back, gz, gh,
+    send_sem, recv_sem,
+):
+    y, x, c, z = position()
+    quarter = 2 * x + c
+    enter(y, x, c, z)
+    net = Net(send_sem, recv_sem, None)
+    sib, xdev, ydev = device(y, x, 1 - c, z), device(y, 1 - x, c, z), device(1 - y, x, c, z)
+    peers = [(device(y, x, c, lax.rem(z + s, 4)), lax.rem(z + s, 4)) for s in (1, 3, 2)]
+    half = gr.shape[1] // 2
+    h1, h2 = pl.ds(0, half), pl.ds(half, half)
+    d1, d2 = pl.ds(0, 384), pl.ds(384, 384)
+    own_rows = rows_of(quarter * ROWS, ROWS)
+    got_x, got_mask, got_back = net.land(), net.land(), net.land()
+    net.local(xs.at[own_rows], xb, got_x)
+    owner = device(y, lax.rem(z, 2), lax.div(z, 2), quarter)
+    is_owner = (lax.rem(z, 2) == x) & (lax.div(z, 2) == c) & (quarter == z)
+    net.send(masks, mask_rows, owner, got_mask, is_owner)
+
+    def tok_of(b, core):
+        return (b // 2) * 4 + (b % 2) * 2 + core
+
+    def blk(t):
+        return rows_of(t * 96, 96)
+
+    def big(t):
+        return rows_of(t * 384, 384)
+
+    fa_in, fb_in, fc_in = net.land(2), net.land(2), net.land()
+    flip = quarter + 1 - 2 * c
+    cross = 2 - 4 * x
+    for i, q in enumerate((flip + cross, flip)):
+        net.send(d_first.at[rows_of(q * ROWS, ROWS)], fb.at[i], sib, fb_in + i)
+    for i, q in enumerate((quarter + cross, quarter)):
+        net.local(d_first.at[rows_of(q * ROWS, ROWS)], fa.at[i], fa_in + i)
+
+    qa_in, qb_in = net.land(4), net.land(4)
+    for b in range(4):
+        net.send(gq.at[blk(tok_of(b, 1 - c))], rq.at[b], sib, qb_in + b)
+        net.local(gq.at[blk(tok_of(b, c))], pq.at[b], qa_in + b)
+    ra_in, rb_in, da_in, db_in = net.land(4), net.land(4), net.land(4), net.land(4)
+    for b in range(4):
+        net.send(gr.at[blk(tok_of(b, 1 - c))], rr.at[b], sib, rb_in + b)
+        net.local(gr.at[blk(tok_of(b, c))], pr.at[b], ra_in + b)
+        net.send(gd.at[big(tok_of(b, 1 - c))], rd.at[b], sib, db_in + b)
+        net.local(gd.at[big(tok_of(b, c))], pd.at[b], da_in + b)
+
+    gz_in = net.land(4)
+    for peer, pz in peers:
+        net.send(gain_part, gz.at[z], peer, gz_in + z)
+    net.local(gain_part, gz.at[z], gz_in + z)
+
+    for i in range(2):
+        net.wait(fa.at[i], fa_in + i)
+        net.wait(fb.at[i], fb_in + i)
+        add_into(fa.at[i], fb.at[i], 256)
+        if i == 0:
+            net.send(fa.at[0], fc, xdev, fc_in)
+
+    first_core = c == 0
+    for b in range(4):
+        net.wait(pq.at[b], qa_in + b)
+        net.wait(rq.at[b], qb_in + b)
+        for part in range(3):
+            own = pq[b, :, 256 * part : 256 * part + 256].astype(F32)
+            new = rq[b, :, 256 * part : 256 * part + 256].astype(F32)
+            left, right = jnp.where(first_core, own, new), jnp.where(first_core, new, own)
+            base = 384 * part
+            hq[b, :, base : base + 128] = left[:, 0:128].astype(BF)
+            hq[b, :, base + 128 : base + 256] = (left[:, 128:256] + right[:, 0:128]).astype(BF)
+            hq[b, :, base + 256 : base + 384] = right[:, 128:256].astype(BF)
+    qy_in, qx_in = net.land(2), net.land()
+    for side in range(2):
+        net.send(hq.at[2 * (1 - y) + side], ryq.at[side], ydev, qy_in + side)
+
+    for b in range(4):
+        net.wait(pr.at[b], ra_in + b)
+        net.wait(rr.at[b], rb_in + b)
+        add_into(pr.at[b], rr.at[b], 384)
+        net.wait(pd.at[b], da_in + b)
+        net.wait(rd.at[b], db_in + b)
+        add_into(pd.at[b], rd.at[b], 128)
+    y_in, x_in, x2_in, y2_in = net.land(2), net.land(), net.land(2), net.land()
+    v_in, u_in, u2_in, v2_in = net.land(2), net.land(), net.land(2), net.land()
+    for side in range(2):
+        net.send(pr.at[2 * (1 - y) + side, :, h1], ry1.at[side], ydev, y_in + side)
+        net.send(pr.at[2 * side + 1 - x, :, h2], rx2.at[side], xdev, x2_in + side)
+    for side in range(2):
+        net.send(pd.at[2 * (1 - y) + side, :, d1], dy1.at[side], ydev, v_in + side)
+        net.send(pd.at[2 * side + 1 - x, :, d2], dx2.at[side], xdev, u2_in + side)
+
+    for side in range(2):
+        net.wait(ryq.at[side], qy_in + side)
+        add_into(hq.at[2 * y + side], ryq.at[side], 384)
+    net.send(hq.at[2 * y + 1 - x], rxq, xdev, qx_in)
+
+    for side in range(2):
+        net.wait(ry1.at[side], y_in + side)
+        add_into(pr.at[2 * y + side, :, h1], ry1.at[side], 384)
+        net.wait(rx2.at[side], x2_in + side)
+        add_into(pr.at[2 * side + x, :, h2], rx2.at[side], 384)
+    net.send(pr.at[2 * y + 1 - x, :, h1], rx1, xdev, x_in)
+    net.send(pr.at[2 * (1 - y) + x, :, h2], ry2, ydev, y2_in)
+    for side in range(2):
+        net.wait(dy1.at[side], v_in + side)
+        add_into(pd.at[2 * y + side, :, d1], dy1.at[side], 128)
+        net.wait(dx2.at[side], u2_in + side)
+        add_into(pd.at[2 * side + x, :, d2], dx2.at[side], 128)
+    net.send(pd.at[2 * y + 1 - x, :, d1], dx1, xdev, u_in)
+    net.send(pd.at[2 * (1 - y) + x, :, d2], dy2, ydev, v2_in)
+
+    net.wait(xb, got_x)
+    net.wait(fc, fc_in)
+    d_zn = fa[1].astype(F32) + fc[...].astype(F32)
+    normed, scale = normalise(xb[...].astype(F32))
+    d_x = dh[...] + scale * (
+        d_zn
+        - jnp.mean(d_zn, axis=-1, keepdims=True)
+        - normed * jnp.mean(d_zn * normed, axis=-1, keepdims=True)
+    )
+    back[...] = d_x.astype(BF)
+    net.send(back, d_rows, owner, got_back, is_owner)
+
+    net.wait(rxq, qx_in)
+    fq[:, lanes_of(1152 * x, 1152)] = hq[2 * y + x]
+    fq[:, lanes_of(1152 * (1 - x), 1152)] = rxq[...]
+    split_rows(fq, spq, 384)
+    zq_in = net.land(4)
+    for peer, pz in peers:
+        net.send(spq.at[pz], rzq.at[z], peer, zq_in + z)
+    net.local(spq.at[z], rzq.at[z], zq_in + z)
+
+    net.wait(rx1, x_in)
+    add_into(pr.at[2 * y + x, :, h1], rx1, 384)
+    net.wait(ry2, y2_in)
+    add_into(pr.at[2 * y + x, :, h2], ry2, 384)
+    split_rows(pr.at[2 * y + x], sp, 384)
+    zr_in, zd_in = net.land(4), net.land(4)
+    for peer, pz in peers:
+        net.send(sp.at[pz], rz.at[z], peer, zr_in + z)
+    net.local(sp.at[z], rz.at[z], zr_in + z)
+    net.wait(dx1, u_in)
+    add_into(pd.at[2 * y + x, :, d1], dx1, 128)
+    net.wait(dy2, v2_in)
+    add_into(pd.at[2 * y + x, :, d2], dy2, 128)
+    for peer, pz in peers:
+        net.send(pd.at[2 * y + x, rows_of(96 * pz, 96)], rzd.at[z], peer, zd_in + z)
+    net.local(pd.at[2 * y + x, rows_of(96 * z, 96)], rzd.at[z], zd_in + z)
+
+    gain_sum[...] = jnp.zeros_like(gain_sum)
+    for part in range(4):
+        net.wait(gz.at[part], gz_in + part)
+        gain_sum[...] += gz[part]
+    gh_in = net.land(3)
+    for i, to in enumerate((xdev, ydev, sib)):
+        gh[i] = gain_sum[...]
+        net.send(gh.at[i], gh.at[3 + i], to, gh_in + i)
+        net.wait(gh.at[3 + i], gh_in + i)
+        gain_sum[...] += gh[3 + i]
+
+    for part in range(4):
+        net.wait(rzq.at[part], zq_in + part)
+    sum_parts(rzq, sum_q, 384)
+    for part in range(4):
+        net.wait(rz.at[part], zr_in + part)
+    sum_parts(rz, sum_r, 384)
+    for part in range(4):
+        net.wait(rzd.at[part], zd_in + part)
+    sum_parts(rzd, sum_d, 256)
+    net.wait(mask_rows, got_mask)
+    net.wait(d_rows, got_back)
+    net.finish()
+
+
+VMEM_SPEC = pl.BlockSpec(memory_space=pltpu.VMEM)
+ANY_SPEC = pl.BlockSpec(memory_space=pl.ANY)
+
+
+def call(body, ident, specs, outs, scratch, sems, args, cost):
+    out_shape = tuple(jax.ShapeDtypeStruct(shape, kind) for shape, kind, _ in outs)
+    scratch_shapes = [pltpu.VMEM(shape, kind) for shape, kind in scratch]
+    if sems:
+        scratch_shapes += [pltpu.SemaphoreType.DMA((n,)) for n in sems]
+    extra = {} if ident is None else dict(collective_id=ident, has_side_effects=True)
+    return pl.pallas_call(
+        body,
+        out_shape=out_shape,
+        in_specs=list(specs),
+        out_specs=tuple(spec for _, _, spec in outs),
+        scratch_shapes=scratch_shapes,
+        compiler_params=pltpu.CompilerParams(vmem_limit_bytes=60 * 2**20, **extra),
+        cost_estimate=pl.CostEstimate(flops=cost, bytes_accessed=2**24, transcendentals=0),
+    )(*args)
+
+
+def home_plan(
+    patches,
+    classes,
+    slot_lengths,
+    w_qkv,
+    w_out,
+    w_up,
+    w_down,
+    w_patch,
+    w_class,
+    norm1,
+    norm2,
+    mask_gain,
+    d_masks,
+):
+    V, A = VMEM_SPEC, ANY_SPEC
+    xin = jnp.concatenate([patches, jnp.pad(classes, ((0, CLS - REAL), (0, 0)))], axis=0)
+    pad_cols = ((0, 0), (0, 0), (0, CLS - REAL))
+    dmx = jnp.pad(d_masks.reshape(PATCH, 2, REAL), pad_cols).reshape(PATCH, 2 * CLS)
+    dmx = jnp.pad(dmx, ((0, 0), (0, 256 - 2 * CLS))).astype(BF)
+    gain = jnp.pad(mask_gain.reshape(1, 2, REAL), pad_cols).reshape(1, 2 * CLS)
+    gain = jnp.pad(gain, ((0, 7), (0, 256 - 2 * CLS)))
+    aux = jnp.broadcast_to(jnp.pad(slot_lengths.reshape(2, 1), ((0, 6), (0, 0))), (8, 128))
+    g1, g2 = norm1.astype(F32)[:, None], norm2.astype(F32)[:, None]
+    wqa = (w_qkv.astype(F32) * g1).astype(BF).reshape(24, 3, 2, 384)
+    wqa = jnp.transpose(wqa, (0, 2, 1, 3)).reshape(24, 2304)
+    wra = jnp.concatenate([(w_up.astype(F32) * g2).astype(BF), w_out, w_patch, w_class], axis=1)
+    wide = wra.shape[1]
+    xs, dmh, auxh, wq, wr, wdn = call(
+        gather_kernel,
+        1,
+        [V, V, V, V, V, A],
+        [
+            ((SLOT_ROWS, 768), BF, A),
+            ((PATCH, 256), BF, A),
+            ((8, 128), jnp.int32, A),
+            ((768, 1152), BF, A),
+            ((768, wide), BF, A),
+            ((3072, 768), BF, A),
+        ],
+        [
+            ((4, 24, 2304), BF),
+            ((4, 24, wide), BF),
+            ((96, 2304), BF),
+            ((96, wide), BF),
+        ],
+        (80, 100),
+        (xin, dmx, aux, wqa, wra, w_down),
+        0,
+    )
+    wp, zn, qr, kr, vr, out, stats = call(
+        forward_kernel,
+        None,
+        [V] * 3,
+        [((768, 768), BF, V), ((SLOT_ROWS, 768), BF, V)]
+        + [((SLOT_ROWS, 256), BF, V)] * 4
+        + [((SLOT_ROWS, 128), F32, V)],
+        [((3, SLOT_ROWS, 256), BF)] * 2,
+        (),
+        (xs, wq, auxh),
+        10**10,
+    )
+    gr, gd, dh, d_out, masks, gain_part = call(
+        middle_kernel,
+        2,
+        [A, V, A, A, V, V, V],
+        [
+            ((768, wide), BF, V),
+            ((3072, 768), BF, V),
+            ((ROWS, 768), F32, V),
+            ((SLOT_ROWS, 256), BF, V),
+            ((PATCH, 256), BF, V),
+            ((8, 256), F32, V),
+        ],
+        [
+            ((768, wide), BF),
+            ((3072, 768), BF),
+            ((ROWS, 768), BF),
+            ((4, ROWS, 256), BF),
+            ((ROWS, 768), BF),
+            ((768, ROWS), BF),
+            ((ROWS, 768), BF),
+            ((ROWS, 3072), BF),
+            ((ROWS, 3072), F32),
+            ((ROWS, 3072), BF),
+            ((ROWS, 768), F32),
+            ((ROWS, 768), F32),
+            ((ROWS, 768), BF),
+            ((PATCH, 768), F32),
+            ((4 * CLS, 768), BF),
+            ((4 * CLS, 768), BF),
+            ((4, CLS, 768), BF),
+            ((ROWS, 768), BF),
+            ((ROWS, 128), F32),
+        ],
+        (24, 24),
+        (xs, out, wr, wdn, dmh, auxh, gain),
+        10**10,
+    )
+    gq, d_first = call(
+        backward_kernel,
+        None,
+        [V] * 9,
+        [((768, 768), BF, V), ((SLOT_ROWS, 768), BF, V)],
+        [
+            ((128, SLOT_ROWS), F32),
+            ((8, SLOT_ROWS), F32),
+            ((SLOT_ROWS, 256), F32),
+            ((SLOT_ROWS, 768), BF),
+            ((768, SLOT_ROWS), BF),
+        ],
+        (),
+        (zn, qr, kr, vr, out, stats, d_out, wp, auxh),
+        10**10,
+    )
+    d_rows, mask_rows, sum_q, sum_r, sum_d, gain_sum = call(
+        reduce_kernel,
+        3,
+        [A, A, A, A, V, A, A, V],
+        [
+            ((ROWS, 768), BF, A),
+            ((PATCH, 256), BF, A),
+            ((24, 2304), F32, V),
+            ((24, wide), F32, V),
+            ((96, 768), F32, V),
+            ((8, 256), F32, V),
+        ],
+        [
+            ((ROWS, 768), BF),
+            ((4, 96, wide), BF),
+            ((4, 384, 768), BF),
+            ((4, 96, wide), BF),
+            ((4, 384, 768), BF),
+            ((2, 96, wide // 2), BF),
+            ((96, wide // 2), BF),
+            ((2, 96, wide // 2), BF),
+            ((96, wide // 2), BF),
+            ((2, 384, 384), BF),
+            ((384, 384), BF),
+            ((2, 384, 384), BF),
+            ((384, 384), BF),
+            ((4, 24, wide), BF),
+            ((4, 24, wide), BF),
+            ((4, 96, 768), BF),
+            ((4, 96, 768), BF),
+            ((4, 96, 768), BF),
+            ((4, 96, 1152), BF),
+            ((2, 96, 1152), BF),
+            ((96, 1152), BF),
+            ((96, 2304), BF),
+            ((4, 24, 2304), BF),
+            ((4, 24, 2304), BF),
+            ((2, ROWS, 768), BF),
+            ((2, ROWS, 768), BF),
+            ((ROWS, 768), BF),
+            ((ROWS, 768), BF),
+            ((4, 8, 256), F32),
+            ((6, 8, 256), F32),
+        ],
+        (60, 90),
+        (gr, gd, gq, d_first, dh, xs, masks, gain_part),
+        0,
+    )
+
+    def unpad(values):
+        return values[:, 0 : 2 * CLS].reshape(-1, 2, CLS)[:, :, 0:REAL].reshape(-1, 2 * REAL)
+
+    d_rows = d_rows.astype(F32)
+    sum_q = jnp.transpose(sum_q.reshape(24, 2, 3, 384), (0, 2, 1, 3)).reshape(24, 2304)
+    sum_up = sum_r[:, 0:3072]
+    return (
+        unpad(mask_rows).astype(F32),
+        d_rows[0:PATCH],
+        d_rows[PATCH : PATCH + REAL],
+        sum_q * g1,
+        sum_r[:, 3072:3840],
+        sum_up * g2,
+        sum_d,
+        sum_r[:, 3840:4608],
+        sum_r[:, 4608:5376],
+        jnp.sum(sum_q * w_qkv.astype(F32), axis=1),
+        jnp.sum(sum_up * w_up.astype(F32), axis=1),
+        unpad(gain_sum[0:1])[0],
+    )
+
+
 def solution(mesh):
     placed = (
         P(("tok", "head"), None),
@@ -269,8 +1264,9 @@
         P(),
         P(("tok", "head"), None),
     )
+    fits = mesh.shape["tok"] == 8 and mesh.shape["head"] == 4
     return jax.shard_map(
-        per_device,
+        home_plan if fits else per_device,
         mesh=mesh,
         in_specs=placed,
         out_specs=(

time: 1150 us -> 396 us (0.34)
  waiting for transfers between devices: 688 us -> 0 us
  Pallas kernels: 0 us -> 374 us
  blocking collectives: 178 us -> 0 us
  matrix products: 108 us -> 0 us
  local copies, waits for them, and re-layouts: 110 us -> 12.1 us
  between operations: 17.4 us -> 0.86 us
  other arithmetic: 25.1 us -> 8.75 us
  starting transfers between devices: 15.7 us -> 0 us
    reduce_scatter x6 -> x0, waiting for transfers between devices: 450 us -> none  [the longest x1 139 us: per_device(): lax.psum_scatter(flat_rows(grad_down_w), ('tok', 'head'), scatter_dimensi...]
    pallas_call x0 -> x5, Pallas kernels: none -> 374 us  [call(): pl.pallas_call(body, out_shape=out_shape, in_specs=list(specs), out_specs...]
    all_gather x6 -> x0, waiting for transfers between devices: 172 us -> none  [the longest x1 51.3 us: per_device(): lax.all_gather(shards[3], ('tok', 'head'), axis=0, tiled=True)]
    dot_general x42 -> x0, matrix products: 108 us -> none  [the longest x16 41.1 us: dot_right_t(): lax.dot_general(left, right, (((1,), (1,)), ((), ())), preferred_element_...]
    unnamed x3 -> x0, blocking collectives: 98.7 us -> none
    all_to_all x1 -> x0, blocking collectives: 64 us -> none  [per_device(): lax.all_to_all(d_moved, 'head', split_axis=0, concat_axis=2, tiled=True)]
    all_to_all x3 -> x0, waiting for transfers between devices: 63.4 us -> none  [the longest x1 39.5 us: per_device(): lax.all_to_all(qkv_rows, 'head', split_axis=2, concat_axis=0, tiled=True)]
    reshape x17 -> x10, local copies, waits for them, and re-layouts: 52.1 us -> 2.18 us  [the longest x2 0.84 us: home_plan(): gain = jnp.pad(mask_gain.reshape(1, 2, REAL), pad_cols).reshape(1, 2 * CLS)]
  transfers between devices with their start and end apart: 16 -> 0, of which waited for: 12 -> 0; matrix products, arithmetic and copies ran while one was open for 20% -> 0% of each run, Pallas kernels for 0% -> 0%
where the time goes in v1:
time: 396 us; the launch traced here: 395 us
  Pallas kernels  374 us (94%)
  local copies, waits for them, and re-layouts  12.1 us (3%)
  other arithmetic  8.75 us (2%)
    pallas_call x5, Pallas kernels, call(): pl.pallas_call(body, out_shape=out_shape, in_specs=list(specs), out_specs...  374 us

profile of v1, /device:TPU:0, one launch (start us, length us, event | category | flops | bytes accessed | tf_op | source)
XLA Modules:
  0.0 395.3 jit_solution(11744012474217580612)
XLA Ops:
  0.7 0.7 convert_element_type.41
  1.4 0.7 convert_element_type.44
  2.1 0.7 pad_bitcast_fusion
  2.8 0.8 reshape.69
  3.6 0.7 broadcast_in_dim.10.aux
  4.3 0.6 pad.31.gain
  4.9 0.9 convert.9
  5.8 0.1 copy.32
  6.0 0.7 pad.28.dmx
  6.6 1.0 fusion.4
  7.7 0.7 reshape.68.wqa
  8.5 0.1 fusion.2
  8.6 0.7 pad_maximum_fusion.wra
  9.3 0.8 fusion.1.xin
  10.1 121.3 %shard_map.220 = (bf16[1344,768]{1,0:T(8,128)(2,1)}, bf16[256,256]{1,0:T(8,128)(2,1)}, s32[8,128]{1,0:T(8,128)}, bf16[768,1152]{1,0:T(8,128)(2,1)}, bf16[768,537...) custom-call(bf16[336,768]{1,0:T(8,128)(2,1)} %fusion.1.xin, bf16[256,256]{1,0:T(8,128)(2,1)} %pad.28.dmx, ...), custom_call_target="tpu_custom_call" | custom-call | bytes 16777216 | tf_op jit(solution)/shard_map/pallas_call | solution.py:1054
  131.4 24.5 %shard_map.221 = (bf16[768,768]{1,0:T(8,128)(2,1)}, bf16[1344,768]{1,0:T(8,128)(2,1)}, bf16[1344,256]{1,0:T(8,128)(2,1)}, bf16[1344,256]{1,0:T(8,128)(2,1)}, bf1...) custom-call(bf16[1344,768]{1,0:T(8,128)(2,1)} %get-tuple-element.39.xs, ...), custom_call_target="tpu_custom_call" | custom-call | flops 10000000000 | bytes 16777216 | tf_op jit(solution)/shard_map/pallas_call | solution.py:1054
  155.9 65.9 %shard_map.222 = (bf16[768,5376]{1,0:T(8,128)(2,1)}, bf16[3072,768]{1,0:T(8,128)(2,1)}, f32[336,768]{1,0:T(8,128)}, bf16[1344,256]{1,0:T(8,128)(2,1)}, bf16[256,256]{1,0:T(8,128)(2,1)}, /*index=5*/f32[8,256]{1,0:T(8,128)}) custom-call(bf16[1344,768]{1,0:T(8,128)(2,1)} %get-tuple-element.39.xs, bf16[1344,256]{1,0:T(8,128)(2,1)} %get-tuple-element.42.o_mine.out, ...), custom_call_target="tpu_custom_call" | custom-call | flops 10000000000 | bytes 16777216 | tf_op jit(solution)/shard_map/pallas_call | solution.py:1054
  221.8 35.6 %shard_map.223 = (bf16[768,768]{1,0:T(8,128)(2,1)}, bf16[1344,768]{1,0:T(8,128)(2,1)}) custom-call(bf16[1344,768]{1,0:T(8,128)(2,1)} %get-tuple-element.48.zn, bf16[1344,256]{1,0:T(8,128)(2,1)} %get-tuple-element.49.qr, bf16[1344,256]{1,0:T(8,128)(2,1)} %get-tuple-element.50.kr, bf16[1344,256]{1,0:T(8,128)(2,1)} %get-tuple-element.51.vr, ...), custom_call_target="tpu_custom_call" | custom-call | flops 10000000000 | bytes 16777216 | tf_op jit(solution)/shard_map/pallas_call | solution.py:1054
  257.5 126.3 %shard_map.224 = (bf16[336,768]{1,0:T(8,128)(2,1)}, bf16[256,256]{1,0:T(8,128)(2,1)}, f32[24,2304]{1,0:T(8,128)}, f32[24,5376]{1,0:T(8,128)}, f32[96,768]{1,0:T(8,128)}, /*index=5*/f32[8,256]{1,0:T(8,128)}) custom-call(bf16[768,5376]{1,0:T(8,128)(2,1)} %get-tuple-element.46.gr, bf16[3072,768]{1,0:T(8,128)(2,1)} %get-tuple-element.47.gd, ...), custom_call_target="tpu_custom_call" | custom-call | bytes 16777216 | tf_op jit(solution)/shard_map/pallas_call | solution.py:1054
  383.8 1.1 copy.34
  384.9 0.7 slice_reduce_fusion
  385.7 0.6 squeeze_reshape.3
  386.3 0.7 reshape.75
  387.0 1.6 fusion.6
  388.7 2.4 fusion.3
  391.1 0.7 slice.44
  391.8 0.9 slice.43
  392.7 0.1 reshape.72
  392.9 0.1 copy.35
  393.0 0.2 reshape.73
  393.2 1.4 fusion.5
  394.6 0.7 copy.39
  (28 shorter events, 0.3 us)
Async XLA Ops:
  0.6 7.8 %copy-start.1 = (bf16[24,3072]{1,0:T(8,128)(2,1)S(1)}, bf16[24,3072]{1,0:T(8,128)(2,1)}, u32[]{:S(2)}) copy-start(bf16[24,3072]{1,0:T(8,128)(2,1)} %param.18) | copy-start | bytes 442372
  0.7 7.9 %copy-start.7 = (bf16[24,768]{1,0:T(8,128)(2,1)S(1)}, bf16[24,768]{1,0:T(8,128)(2,1)}, u32[]{:S(2)}) copy-start(bf16[24,768]{1,0:T(8,128)(2,1)} %param.21) | copy-start | bytes 110596
  0.7 7.9 %copy-start.8 = (bf16[24,768]{1,0:T(8,128)(2,1)S(1)}, bf16[24,768]{1,0:T(8,128)(2,1)}, u32[]{:S(2)}) copy-start(bf16[24,768]{1,0:T(8,128)(2,1)} %param.20) | copy-start | bytes 110596
  0.7 7.9 %copy-start.9 = (bf16[24,768]{1,0:T(8,128)(2,1)S(1)}, bf16[24,768]{1,0:T(8,128)(2,1)}, u32[]{:S(2)}) copy-start(bf16[24,768]{1,0:T(8,128)(2,1)} %param.17) | copy-start | bytes 110596
  0.7 8.6 %copy-start.6 = (bf16[75,768]{1,0:T(8,128)(2,1)S(1)}, bf16[75,768]{1,0:T(8,128)(2,1)}, u32[]{:S(2)}) copy-start(bf16[75,768]{1,0:T(8,128)(2,1)} %param.14) | copy-start | bytes 345604
  0.7 8.6 %copy-start.3 = (bf16[256,768]{1,0:T(8,128)(2,1)S(1)}, bf16[256,768]{1,0:T(8,128)(2,1)}, u32[]{:S(2)}) copy-start(bf16[256,768]{1,0:T(8,128)(2,1)} %param.13) | copy-start | bytes 1179652
  383.8 7.3 %copy-start = (bf16[336,768]{1,0:T(8,128)(2,1)S(1)}, bf16[336,768]{1,0:T(8,128)(2,1)}, u32[]{:S(2)}) copy-start(bf16[336,768]{1,0:T(8,128)(2,1)} %get-tuple-element.61) | copy-start | bytes 1548292
  383.8 8.9 %copy-start.5 = (f32[24,2304]{1,0:T(8,128)S(1)}, f32[24,2304]{1,0:T(8,128)}, u32[]{:S(2)}) copy-start(f32[24,2304]{1,0:T(8,128)} %get-tuple-element.62) | copy-start | bytes 663556
  388.7 4.5 %copy-start.2 = (bf16[24,2304]{1,0:T(8,128)(2,1)S(1)}, bf16[24,2304]{1,0:T(8,128)(2,1)}, u32[]{:S(2)}) copy-start(bf16[24,2304]{1,0:T(8,128)(2,1)} %param.16) | copy-start | bytes 331780
  391.1 3.5 copy-start.4

commit v2 on v0

--- a/solution.py
+++ b/solution.py
@@ -1,6 +1,8 @@
 import jax
 import jax.numpy as jnp
 from jax import lax
+from jax.experimental import pallas as pl
+from jax.experimental.pallas import tpu as pltpu
 from jax.sharding import PartitionSpec as P
 
 HEADS = 12
@@ -253,6 +255,1140 @@
     )
 
 
+ROWS = 336
+SLOT_ROWS = 4 * ROWS
+PATCH = 256
+CLS = 80
+REAL = 75
+PIECE = 80
+LEAD = 16
+MESH = pl.DeviceIdType.MESH
+BF = jnp.bfloat16
+F32 = jnp.float32
+
+
+def position():
+    tok = lax.axis_index("tok")
+    return lax.div(tok, 4), lax.rem(lax.div(tok, 2), 2), lax.rem(tok, 2), lax.axis_index("head")
+
+
+def device(y, x, c, z):
+    return {"tok": y * 4 + x * 2 + c, "head": z}
+
+
+def enter(y, x, c, z):
+    barrier = pltpu.get_barrier_semaphore()
+    others = [device(1 - y, x, c, z)]
+    for turn in range(1, 16):
+        flip_x, flip_c, step = turn // 8, (turn // 4) % 2, turn % 4
+        others.append(
+            device(
+                y,
+                1 - x if flip_x else x,
+                1 - c if flip_c else c,
+                lax.rem(z + step, 4),
+            )
+        )
+    for other in others:
+        pl.semaphore_signal(barrier, inc=1, device_id=other, device_id_type=MESH)
+    pl.semaphore_wait(barrier, len(others))
+
+
+class Net:
+    def __init__(self, send_sem, recv_sem, here):
+        self.send_sem, self.recv_sem, self.here = send_sem, recv_sem, here
+        self.sends, self.recvs, self.open = 0, 0, []
+
+    def land(self, count=1):
+        first = self.recvs
+        self.recvs += count
+        return first
+
+    def send(self, src, dst, to, slot, skip=None):
+        index = self.sends
+        self.sends += 1
+        copy = pltpu.make_async_remote_copy(
+            src_ref=src,
+            dst_ref=dst,
+            send_sem=self.send_sem.at[index],
+            recv_sem=self.recv_sem.at[slot],
+            device_id=to,
+            device_id_type=MESH,
+        )
+        if skip is None:
+            copy.start()
+            self.open.append((copy, None))
+        else:
+            pl.when(jnp.logical_not(skip))(copy.start)
+            self.open.append((copy, skip))
+
+            @pl.when(skip)
+            def _():
+                pltpu.make_async_copy(src, dst, self.recv_sem.at[slot]).start()
+
+    def local(self, src, dst, slot):
+        pltpu.make_async_copy(src, dst, self.recv_sem.at[slot]).start()
+
+    def wait(self, ref, slot):
+        pltpu.make_async_copy(ref, ref, self.recv_sem.at[slot]).wait()
+
+    def finish(self):
+        for copy, skip in self.open:
+            if skip is None:
+                copy.wait_send()
+            else:
+                pl.when(jnp.logical_not(skip))(copy.wait_send)
+        self.open = []
+
+
+def rows_of(start, size):
+    return pl.ds(pl.multiple_of(start, 16), size)
+
+
+def lanes_of(start, size):
+    return pl.ds(pl.multiple_of(start, 128), size)
+
+
+def nn(left, right):
+    return jnp.dot(left, right, preferred_element_type=F32)
+
+
+def nt(left, right):
+    return lax.dot_general(left, right, (((1,), (1,)), ((), ())), preferred_element_type=F32)
+
+
+def tn(left, right):
+    return lax.dot_general(left, right, (((0,), (0,)), ((), ())), preferred_element_type=F32)
+
+
+def segments(row, lead_len, tail_len):
+    source = (
+        (row >= ROWS).astype(jnp.int32)
+        + (row >= 2 * ROWS).astype(jnp.int32)
+        + (row >= 3 * ROWS).astype(jnp.int32)
+    )
+    offset = row - source * ROWS
+    patch = source * PATCH + offset
+    patch_seg = jnp.where(patch < lead_len, 0, jnp.where(patch < lead_len + tail_len, 1, -1))
+    number = offset - PATCH
+    class_seg = jnp.where(source >= 2, 1, 0)
+    filler = number >= REAL
+    seg = jnp.where(offset < PATCH, patch_seg, jnp.where(filler, -1, class_seg))
+    return seg, filler
+
+
+def normalise(values):
+    centre = values - jnp.mean(values, axis=-1, keepdims=True)
+    scale = lax.rsqrt(jnp.mean(centre * centre, axis=-1, keepdims=True) + 1e-05)
+    return centre * scale, scale
+
+
+def own_lanes(c, head, shape):
+    lane = lax.broadcasted_iota(jnp.int32, shape, len(shape) - 1)
+    group = lane // 64 - c
+    if head is None:
+        return (group >= 0) & (group < 3)
+    return group == head
+
+
+def group_of(y, x, c, z):
+    quarter = 2 * x + c
+    return [
+        (device(y, x, 1 - c, z), quarter + 1 - 2 * c),
+        (device(y, 1 - x, c, z), quarter + 2 - 4 * x),
+        (device(y, 1 - x, 1 - c, z), quarter + 3 - 4 * x - 2 * c),
+    ]
+
+
+TILE = 256
+
+
+class Pump:
+    def __init__(self):
+        self.todo = []
+
+    def add(self, step):
+        self.todo.append(step)
+
+    def run(self, count=None):
+        count = len(self.todo) if count is None else min(count, len(self.todo))
+        for step in self.todo[:count]:
+            step()
+        self.todo = self.todo[count:]
+
+
+def join(stage, block, start, size, width):
+    def body(i, carry):
+        cols = lanes_of(start + i * width, width)
+        parts = [stage[src, :, cols].astype(F32) for src in range(4)]
+        block[:, cols] = jnp.concatenate(parts, axis=0).astype(BF)
+        return carry
+
+    lax.fori_loop(0, size // width, body, 0)
+
+
+OUT_AT, UP_AT, PATCH_AT, CLASS_AT = 0, 768, 3840, 4608
+
+
+def front_kernel(
+    xin, dmx, aux_in, wqa, wra, wd_in, gain,
+    gr_o, gd_o, dh, dob, masks, gain_part, zn_o, qr_o, kr_o, vr_o, out_o, stats_o, wp_o, xb_o, aux_o,
+    xs, zn, qr, kr, vr, out, stats, wp, wq, wr, wd, stq, str_, bq, pool0, pool1,
+    gr, gd, dmh, aux, obuf, att, znt, zn2, h_f, dz_f, dzb, pp_f, cn, dcn, dcbuf, inv,
+    send_sem, recv_sem,
+):
+    y, x, c, z = position()
+    tok = y * 4 + x * 2 + c
+    quarter = 2 * x + c
+    enter(y, x, c, z)
+    net = Net(send_sem, recv_sem, None)
+    sib, xdev, ydev = device(y, x, 1 - c, z), device(y, 1 - x, c, z), device(1 - y, x, c, z)
+    flip = 1 - 2 * c
+    t_x, t_y = tok + 2 - 4 * x, tok + 4 - 8 * y
+    t_xy = t_x + 4 - 8 * y
+    other = quarter + 2 - 4 * x
+    peers = [device(y, x, c, lax.rem(z + step, 4)) for step in (1, 3, 2)]
+    outs = []
+
+    def store(src, dst):
+        slot = net.land()
+        net.local(src, dst, slot)
+        outs.append((dst, slot))
+
+    home = 2 * c + x
+    got_lead, got_piece, got_dm, got_aux = net.land(4), net.land(4), net.land(), net.land()
+    for q in (3, 2, 1, 0):
+        to = device(y, q // 2, q % 2, home)
+        mine = (z == home) & (quarter == q)
+        off = LEAD + PIECE * q
+        net.send(
+            xin.at[pl.ds(off, PIECE)],
+            xs.at[rows_of(z * ROWS + off, PIECE)],
+            to,
+            got_piece + z,
+            mine,
+        )
+        net.send(xin.at[pl.ds(0, LEAD)], xs.at[rows_of(z * ROWS, LEAD)], to, got_lead + z, mine)
+    to_home = device(y, lax.div(z, 2), lax.rem(z, 2), home)
+    at_home = (z == home) & (quarter == z)
+    net.send(aux_in, aux, to_home, got_aux, at_home)
+
+    def blk(t):
+        return rows_of(t * 96, 96)
+
+    def big(t):
+        return rows_of(t * 384, 384)
+
+    q_cols = [pl.ds(768 * part, 768) for part in range(3)]
+    got_q = [net.land(4) for _ in range(3)]
+    for part in range(3):
+        net.local(wqa.at[:, q_cols[part]], stq.at[z, :, q_cols[part]], got_q[part] + z)
+        for peer in peers:
+            net.send(wqa.at[:, q_cols[part]], stq.at[z, :, q_cols[part]], peer, got_q[part] + z)
+    chunks = [(OUT_AT, 768), (UP_AT, 1536), (UP_AT + 1536, 1536), ("d", 0), ("d", 256), ("d", 512), (PATCH_AT, 1536)]
+    got_z = [net.land(4) for _ in chunks]
+
+    def raw_send(k):
+        at, size = chunks[k]
+        if at == "d":
+            cols = pl.ds(size, 256)
+            src, dst = wd_in.at[:, cols], wd.at[rows_of((tok * 4 + z) * 96, 96), cols]
+        else:
+            cols = pl.ds(at, size)
+            src, dst = wra.at[:, cols], str_.at[z, :, cols]
+        net.local(src, dst, got_z[k] + z)
+        for peer in peers:
+            net.send(src, dst, peer, got_z[k] + z)
+
+    def piece(source, owner):
+        return xs.at[rows_of(source * ROWS + LEAD + PIECE * owner, PIECE)]
+
+    fwd_s, fwd_x, fwd_xs = net.land(4), net.land(4), net.land(4)
+    for src in range(4):
+        net.wait(piece(src, quarter), got_piece + src)
+        net.send(piece(src, quarter), piece(src, quarter), xdev, fwd_x + src)
+        net.send(piece(src, quarter), piece(src, quarter), sib, fwd_s + src)
+    raw_send(0)
+    raw_send(1)
+
+    q_x, q_y, q_xy, q_s = net.land(3), net.land(3), net.land(3), net.land(12)
+
+    def q_join(part):
+        for src in range(4):
+            net.wait(stq.at[src, :, q_cols[part]], got_q[part] + src)
+        join(stq, bq, 768 * part, 768, 384)
+        own = lanes_of(768 * part + 384 * x, 384)
+        far = lanes_of(768 * part + 384 * (1 - x), 384)
+        cols = pl.ds(384 * part, 384)
+        net.send(bq.at[:, far], wq.at[blk(tok), cols], xdev, q_x + part)
+        net.send(bq.at[:, own], wq.at[blk(tok), cols], ydev, q_y + part)
+        wq[blk(tok), cols] = bq[:, own]
+        net.send(bq.at[:, own], wq.at[blk(tok), cols], sib, q_s + part)
+
+    def q_cross(part):
+        cols = pl.ds(384 * part, 384)
+        ref = wq.at[blk(t_x), cols]
+        net.wait(ref, q_x + part)
+        net.send(ref, ref, ydev, q_xy + part)
+        net.send(ref, ref, sib, q_s + 3 + part)
+
+    def q_last(part):
+        cols = pl.ds(384 * part, 384)
+        net.wait(wq.at[blk(t_y), cols], q_y + part)
+        net.send(wq.at[blk(t_y), cols], wq.at[blk(t_y), cols], sib, q_s + 6 + part)
+        net.wait(wq.at[blk(t_xy), cols], q_xy + part)
+        net.send(wq.at[blk(t_xy), cols], wq.at[blk(t_xy), cols], sib, q_s + 9 + part)
+
+    for part in range(3):
+        q_join(part)
+        if part:
+            q_cross(part - 1)
+    for src in range(4):
+        net.wait(piece(src, other), fwd_x + src)
+        net.send(piece(src, other), piece(src, other), sib, fwd_xs + src)
+    q_cross(2)
+    raw_send(2)
+    net.send(dmx, dmh, to_home, got_dm, at_home)
+
+    sx, sy, ss = [], [], []
+    for _ in chunks:
+        sx.append(net.land(3))
+        sy.append(net.land(3))
+        ss.append(net.land(4))
+
+    def parts(k):
+        at, size = chunks[k]
+        if at == "d":
+            return wd, big, pl.ds(size, 128), pl.ds(size + 128, 128), pl.ds(size, 256)
+        return wr, blk, pl.ds(at, size // 2), pl.ds(at + size // 2, size // 2), pl.ds(at, size)
+
+    def pass_on(ref, to, slot):
+        net.send(ref, ref, to, slot)
+
+    def stage_z(k):
+        def step():
+            at, size = chunks[k]
+            ref, rows, a, b, both = parts(k)
+            for src in range(4):
+                if at == "d":
+                    net.wait(wd.at[rows_of((tok * 4 + src) * 96, 96), both], got_z[k] + src)
+                else:
+                    net.wait(str_.at[src, :, both], got_z[k] + src)
+            if at != "d":
+                join(str_, wr.at[blk(tok)], at, size, 384)
+            pass_on(ref.at[rows(tok), a], xdev, sx[k])
+            pass_on(ref.at[rows(tok), b], ydev, sy[k])
+            pass_on(ref.at[rows(tok), b], xdev, sx[k] + 1)
+            pass_on(ref.at[rows(tok), a], ydev, sy[k] + 1)
+            pass_on(ref.at[rows(tok), both], sib, ss[k])
+            if k + 3 < len(chunks):
+                raw_send(k + 3)
+
+        return step
+
+    def stage_one(k):
+        def step():
+            ref, rows, a, b, both = parts(k)
+            net.wait(ref.at[rows(t_x), a], sx[k])
+            pass_on(ref.at[rows(t_x), a], ydev, sy[k] + 2)
+            net.wait(ref.at[rows(t_y), b], sy[k])
+            pass_on(ref.at[rows(t_y), b], xdev, sx[k] + 2)
+
+        return step
+
+    def stage_two(k):
+        def step():
+            ref, rows, a, b, both = parts(k)
+            net.wait(ref.at[rows(t_x), b], sx[k] + 1)
+            pass_on(ref.at[rows(t_x), both], sib, ss[k] + 1)
+            net.wait(ref.at[rows(t_y), a], sy[k] + 1)
+            pass_on(ref.at[rows(t_y), both], sib, ss[k] + 2)
+
+        return step
+
+    def stage_three(k):
+        def step():
+            ref, rows, a, b, both = parts(k)
+            net.wait(ref.at[rows(t_xy), a], sy[k] + 2)
+            net.wait(ref.at[rows(t_xy), b], sx[k] + 2)
+            pass_on(ref.at[rows(t_xy), both], sib, ss[k] + 3)
+
+        return step
+
+    def ready(k):
+        ref, rows, a, b, both = parts(k)
+        for i, t in enumerate((tok, t_x, t_y, t_xy)):
+            net.wait(ref.at[rows(t + flip), both], ss[k] + i)
+
+    pump = Pump()
+    count = len(chunks)
+    for k in range(count + 2):
+        if k < count:
+            pump.add(stage_z(k))
+        if 0 <= k - 1 < count:
+            pump.add(stage_one(k - 1))
+            pump.add(stage_two(k - 1))
+        if 0 <= k - 2 < count:
+            pump.add(stage_three(k - 2))
+
+    for part in range(3):
+        q_last(part)
+    sibling = quarter + flip
+    for src in range(4):
+        net.wait(xs.at[rows_of(src * ROWS, LEAD)], got_lead + src)
+        net.wait(piece(src, sibling), fwd_s + src)
+        net.wait(piece(src, sibling + 2 - 4 * x), fwd_xs + src)
+    net.wait(aux, got_aux)
+    pump.run(1)
+    for part in range(3):
+        cols = pl.ds(384 * part, 384)
+        for i, t in enumerate((tok, t_x, t_y, t_xy)):
+            net.wait(wq.at[blk(t + flip), cols], q_s + 3 * i + part)
+
+    lead_len, tail_len = aux[0:1, 0:1], aux[1:2, 0:1]
+    keep = own_lanes(c, None, (768, 256))
+    for part in range(3):
+        cols = lanes_of(384 * part + 128 * c, 256)
+        wp[:, 256 * part : 256 * part + 256] = jnp.where(keep, wq[:, cols], 0.0).astype(BF)
+
+    def project(i, carry):
+        rows = rows_of(i * ROWS, ROWS)
+        normed = normalise(xs[rows, :].astype(F32))[0].astype(BF)
+        zn[rows, :] = normed
+        qr[rows, :] = (nn(normed, wp[:, 0:256]).astype(BF) * 0.125).astype(BF)
+        kr[rows, :] = nn(normed, wp[:, 256:512]).astype(BF)
+        vr[rows, :] = nn(normed, wp[:, 512:768]).astype(BF)
+        return carry
+
+    lax.fori_loop(0, 4, project, 0)
+    pump.run(2)
+    for head in range(3):
+        mine = own_lanes(c, head, (SLOT_ROWS, 256))
+        cols = pl.ds(256 * head, 256)
+        pool0[:, cols] = jnp.where(mine, kr[...], 0.0).astype(BF)
+        pool1[:, cols] = jnp.where(mine, vr[...], 0.0).astype(BF)
+    own_rows = rows_of(quarter * ROWS, ROWS)
+    store(zn, zn_o)
+    store(qr, qr_o)
+    store(kr, kr_o)
+    store(vr, vr_o)
+    store(wp, wp_o)
+    store(xs.at[own_rows], xb_o)
+    store(aux, aux_o)
+    key_row = lax.broadcasted_iota(jnp.int32, (1, SLOT_ROWS), 1)
+    key_seg, key_filler = segments(key_row, lead_len, tail_len)
+    key_seg = jnp.where(key_seg < 0, -5, key_seg)
+    masked = jnp.where(key_filler, -3e38, -1e30)
+    group = group_of(y, x, c, z)
+    got_o, got_cn, got_dc = net.land(4), net.land(4), net.land(4)
+    lane = lax.broadcasted_iota(jnp.int32, (ROWS, 128), 1)
+    for to, q in group[::-1] + [(None, quarter)]:
+        rows = rows_of(q * ROWS, ROWS)
+        row = lax.broadcasted_iota(jnp.int32, (ROWS, 1), 0) + q * ROWS
+        seg = segments(row, lead_len, tail_len)[0]
+        query = qr[rows, :]
+        total_out = jnp.zeros((ROWS, 256), F32)
+        kept = jnp.zeros((ROWS, 128), F32)
+        for head in range(3):
+            cols = pl.ds(256 * head, 256)
+            scores = jnp.where(seg == key_seg, nt(query, pool0[:, cols]), masked)
+            top = jnp.max(scores, axis=1, keepdims=True)
+            expo = jnp.exp(scores - top)
+            total = jnp.sum(expo, axis=1, keepdims=True)
+            probs = (expo * (1.0 / total)).astype(BF)
+            total_out = total_out + nn(probs, pool1[:, cols])
+            kept = jnp.where(lane == head, top + jnp.log(total), kept)
+            pump.run(2)
+        out[rows, :] = total_out.astype(BF)
+        stats[rows, :] = kept
+        if to is None:
+            net.local(out.at[rows], obuf.at[quarter], got_o + quarter)
+        else:
+            net.send(out.at[rows], obuf.at[quarter], to, got_o + quarter)
+    store(out, out_o)
+    store(stats, stats_o)
+
+    row = lax.broadcasted_iota(jnp.int32, (PATCH, 1), 0) + quarter * ROWS
+    seg = segments(row, lead_len, tail_len)[0]
+    first_image = seg == 0
+    valid = jnp.where(seg >= 0, 1.0, 0.0)
+    for q in range(4):
+        net.wait(obuf.at[q], got_o + q)
+    for side in range(2):
+        a, b = obuf[2 * side], obuf[2 * side + 1]
+        base = 384 * side
+        att[:, base : base + 128] = a[:, 0:128]
+        att[:, base + 128 : base + 256] = a[:, 128:256] + b[:, 0:128]
+        att[:, base + 256 : base + 384] = b[:, 128:256]
+    pump.run()
+    ready(0)
+    w_out = wr.at[:, pl.ds(OUT_AT, 768)]
+    w_patch, w_class = wr.at[:, pl.ds(PATCH_AT, 768)], wr.at[:, pl.ds(CLASS_AT, 768)]
+    h_f[...] = xs[own_rows, :].astype(F32) + nn(att[...], w_out[...])
+    normed, scale = normalise(h_f[...])
+    inv[...] = jnp.broadcast_to(scale, inv.shape)
+    zn2[...] = normed.astype(BF)
+    znt[...] = normed.T.astype(BF)
+    ready(1)
+    ready(2)
+    gl, slope = pool0, pool1
+
+    def panel(i):
+        return rows_of(lax.div(i, 3) * ROWS, ROWS), lanes_of(lax.rem(i, 3) * TILE, TILE)
+
+    def up_step(i, carry):
+        u = nn(zn2[...], wr[:, lanes_of(UP_AT + i * TILE, TILE)])
+        cdf = 0.5 * (1.0 + lax.erf(u * 0.7071067811865476))
+        rows, cols = panel(i)
+        gl[rows, cols] = (u * cdf).astype(BF)
+        slope[rows, cols] = (cdf + u * (jnp.exp(-0.5 * u * u) * 0.3989422804014327)).astype(BF)
+        return carry
+
+    lax.fori_loop(0, 12, up_step, 0)
+    for k in range(3, count):
+        ready(k)
+    mlp = nn(gl[0:ROWS, :], wd[0:768, :])
+    for p in range(1, 4):
+        mlp = mlp + nn(gl[ROWS * p : ROWS * p + ROWS, :], wd[768 * p : 768 * p + 768, :])
+    z2 = (h_f[...] + mlp).astype(BF)
+    z2p, z2c = z2[0:PATCH], z2[PATCH:ROWS]
+
+    def unit(values):
+        return values * lax.rsqrt(jnp.sum(values * values, axis=-1, keepdims=True) + 1e-06)
+
+    def unit_back(values, cot):
+        r = lax.rsqrt(jnp.sum(values * values, axis=-1, keepdims=True) + 1e-06)
+        return r * cot - values * (r * r * r * jnp.sum(values * cot, axis=-1, keepdims=True))
+
+    cc = nn(z2c, w_class[...])
+    own_cls = rows_of(quarter * CLS, CLS)
+    cn[own_cls, :] = unit(cc).astype(BF)
+    for to, q in group:
+        net.send(cn.at[own_cls], cn.at[own_cls], to, got_cn + quarter)
+    pp = nn(z2p, w_patch[...])
+    pp_f[...] = pp
+    pn = unit(pp).astype(BF)
+    net.wait(dmh, got_dm)
+    for to, q in group:
+        net.wait(cn.at[rows_of(q * CLS, CLS)], got_cn + q)
+    low, high = cn[0 : 2 * CLS, :], cn[2 * CLS : 4 * CLS, :]
+    wide = 2 * CLS
+    lane = lax.broadcasted_iota(jnp.int32, (1, wide), 1)
+    real = jnp.where(lane >= CLS, lane - CLS, lane) < REAL
+    raw = jnp.where(first_image, nt(pn, low), nt(pn, high))
+
+    def mean(values):
+        return jnp.sum(jnp.where(real, values, 0.0), axis=1, keepdims=True) * (0.5 / REAL)
+
+    centre = jnp.where(real, raw - mean(raw), 0.0)
+    sigma = lax.rsqrt(mean(centre * centre) + 1e-05)
+    xhat = centre * sigma
+    mask_gain = gain[0:1, 0:wide]
+    dm = dmh[:, 0:wide].astype(F32) * valid
+    dx = jnp.where(real, dm * mask_gain, 0.0)
+    d_raw = jnp.where(real, sigma * (dx - mean(dx) - xhat * mean(dx * xhat)), 0.0)
+    d_low = jnp.where(first_image, d_raw, 0.0).astype(BF)
+    d_high = jnp.where(first_image, 0.0, d_raw).astype(BF)
+    dcn[0:wide, :] = tn(d_low, pn).astype(BF)
+    dcn[wide : 2 * wide, :] = tn(d_high, pn).astype(BF)
+    for to, q in group:
+        net.send(dcn.at[rows_of(q * CLS, CLS)], dcbuf.at[quarter], to, got_dc + quarter)
+    net.local(dcn.at[own_cls], dcbuf.at[quarter], got_dc + quarter)
+    masks[:, wide:256] = jnp.zeros((PATCH, 256 - wide), BF)
+    masks[:, 0:wide] = (xhat * mask_gain * valid).astype(BF)
+    gain_part[...] = jnp.zeros_like(gain_part)
+    gain_part[0:1, 0:wide] = jnp.sum(dm * xhat, axis=0, keepdims=True)
+    d_pn = nn(d_low, low) + nn(d_high, high)
+    d_pp = unit_back(pp_f[...], d_pn).astype(BF)
+    dz_f[0:PATCH, :] = nt(d_pp, w_patch[...])
+    gr[:, PATCH_AT : PATCH_AT + 768] = tn(z2p, d_pp).astype(BF)
+    for q in range(4):
+        net.wait(dcbuf.at[q], got_dc + q)
+    d_cn = dcbuf[0].astype(F32) + dcbuf[1].astype(F32) + dcbuf[2].astype(F32) + dcbuf[3].astype(F32)
+    d_cc = unit_back(cc, d_cn).astype(BF)
+    dz_f[PATCH:ROWS, :] = nt(d_cc, w_class[...])
+    gr[:, CLASS_AT : CLASS_AT + 768] = tn(z2c, d_cc).astype(BF)
+    mask_cols = pl.ds(PATCH_AT, 1536)
+    store(gr.at[:, mask_cols], gr_o.at[:, mask_cols])
+
+    dzb[...] = dz_f[...].astype(BF)
+
+    def down_step(i, carry):
+        rows, cols = panel(i)
+        flat = rows_of(i * TILE, TILE)
+        d_u = (nt(dzb[...], wd[flat, :]) * slope[rows, cols].astype(F32)).astype(BF)
+        slope[rows, cols] = d_u
+        gd[flat, :] = tn(gl[rows, cols], dzb[...]).astype(BF)
+        gr[:, lanes_of(UP_AT + i * TILE, TILE)] = nn(znt[...], d_u).astype(BF)
+        return carry
+
+    lax.fori_loop(0, 12, down_step, 0)
+    store(gd, gd_o)
+    up_cols = pl.ds(UP_AT, 3072)
+    store(gr.at[:, up_cols], gr_o.at[:, up_cols])
+    d_zn = nt(slope[0:ROWS, :], wr[:, UP_AT : UP_AT + 768])
+    for p in range(1, 4):
+        base = UP_AT + 768 * p
+        d_zn = d_zn + nt(slope[ROWS * p : ROWS * p + ROWS, :], wr[:, base : base + 768])
+    normed = h_f[...]
+    normed = (normed - jnp.mean(normed, axis=-1, keepdims=True)) * inv[:, 0:1]
+    d_h = dz_f[...] + inv[:, 0:1] * (
+        d_zn
+        - jnp.mean(d_zn, axis=-1, keepdims=True)
+        - normed * jnp.mean(d_zn * normed, axis=-1, keepdims=True)
+    )
+    dh[...] = d_h
+    d_hb = d_h.astype(BF)
+    dob[...] = nt(d_hb, w_out[...]).astype(BF)
+    gr[:, OUT_AT : OUT_AT + 768] = tn(att[...], d_hb).astype(BF)
+    out_cols = pl.ds(OUT_AT, 768)
+    store(gr.at[:, out_cols], gr_o.at[:, out_cols])
+    for dst, slot in outs:
+        net.wait(dst, slot)
+    net.finish()
+
+
+def add_into(total, part, width):
+    def body(i, carry):
+        cols = lanes_of(i * width, width)
+        total[:, cols] = (total[:, cols].astype(F32) + part[:, cols].astype(F32)).astype(BF)
+        return carry
+
+    lax.fori_loop(0, total.shape[1] // width, body, 0)
+
+
+def split_rows(block, stage, width):
+    def body(i, carry):
+        cols = lanes_of(i * width, width)
+        values = block[:, cols].astype(F32)
+        for part in range(4):
+            stage[part, :, cols] = values[24 * part : 24 * part + 24].astype(BF)
+        return carry
+
+    lax.fori_loop(0, block.shape[1] // width, body, 0)
+
+
+def sum_parts(stage, total, width):
+    def body(i, carry):
+        cols = lanes_of(i * width, width)
+        total[:, cols] = (
+            stage[0, :, cols].astype(F32)
+            + stage[1, :, cols].astype(F32)
+            + stage[2, :, cols].astype(F32)
+            + stage[3, :, cols].astype(F32)
+        )
+        return carry
+
+    lax.fori_loop(0, total.shape[1] // width, body, 0)
+
+
+def back_kernel(
+    gr, gd, zn, qr, kr, vr, out, stats, dob, wp, aux, dh, xb, masks, gain_part,
+    d_rows, mask_rows, sum_q, sum_r, sum_d, gain_sum,
+    pr, pd, rr, rd, ry1, rx1, rx2, ry2, dy1, dx1, dx2, dy2, sp, rz, rzd,
+    gq, rq, hq, ryq, rxq, fq, spq, rzq, d_first, fb, fc, back, gz, gh, kh, vh, dqkv, dk, dv, d_out,
+    send_sem, recv_sem,
+):
+    y, x, c, z = position()
+    quarter = 2 * x + c
+    enter(y, x, c, z)
+    net = Net(send_sem, recv_sem, None)
+    sib, xdev, ydev = device(y, x, 1 - c, z), device(y, 1 - x, c, z), device(1 - y, x, c, z)
+    peers = [(device(y, x, c, lax.rem(z + s, 4)), lax.rem(z + s, 4)) for s in (1, 3, 2)]
+    group = group_of(y, x, c, z)
+    own_rows = rows_of(quarter * ROWS, ROWS)
+
+    got_do = net.land(4)
+
+    def piece(q):
+        return dob.at[:, lanes_of(384 * lax.div(q, 2) + 128 * lax.rem(q, 2), 256)]
+
+    net.local(piece(quarter), d_out.at[own_rows], got_do + quarter)
+    for to, q in group:
+        net.send(piece(q), d_out.at[own_rows], to, got_do + quarter)
+
+    def tok_of(b, core):
+        return (b // 2) * 4 + (b % 2) * 2 + core
+
+    def blk(t):
+        return rows_of(t * 96, 96)
+
+    def big(t):
+        return rows_of(t * 384, 384)
+
+    chunks = [(PATCH_AT, 1536), ("d", 0), ("d", 256), ("d", 512), (UP_AT, 1536), (UP_AT + 1536, 1536), (OUT_AT, 768)]
+    count = len(chunks)
+    own_in = [net.land(4) for _ in chunks]
+    sib_in = [net.land(4) for _ in chunks]
+    y_in = [net.land(3) for _ in chunks]
+    x_in = [net.land(3) for _ in chunks]
+    z_in = [net.land(4) for _ in chunks]
+
+    def parts(k):
+        at, size = chunks[k]
+        if at == "d":
+            return pl.ds(size, 256), pl.ds(size, 128), pl.ds(size + 128, 128), pl.ds(size // 2, 128), 128
+        half = size // 2
+        return pl.ds(at, size), pl.ds(at, half), pl.ds(at + half, half), pl.ds(at // 2, half), 384
+
+    for k in range(count):
+        both = parts(k)[0]
+        for b in range(4):
+            if chunks[k][0] == "d":
+                net.send(gd.at[big(tok_of(b, 1 - c)), both], rd.at[b, :, both], sib, sib_in[k] + b)
+                net.local(gd.at[big(tok_of(b, c)), both], pd.at[b, :, both], own_in[k] + b)
+            else:
+                net.send(gr.at[blk(tok_of(b, 1 - c)), both], rr.at[b, :, both], sib, sib_in[k] + b)
+                net.local(gr.at[blk(tok_of(b, c)), both], pr.at[b, :, both], own_in[k] + b)
+
+    def bufs(k):
+        if chunks[k][0] == "d":
+            return pd, rd, dy1, dx1, dx2, dy2
+        return pr, rr, ry1, rx1, rx2, ry2
+
+    def stage_core(k):
+        def step():
+            both, a, b2, h, width = parts(k)
+            mine, new, y1, x1, x2, y2 = bufs(k)
+            for b in range(4):
+                net.wait(mine.at[b, :, both], own_in[k] + b)
+                net.wait(new.at[b, :, both], sib_in[k] + b)
+                add_into(mine.at[b, :, both], new.at[b, :, both], width)
+            for side in range(2):
+                net.send(mine.at[2 * (1 - y) + side, :, a], y1.at[side, :, h], ydev, y_in[k] + side)
+                net.send(mine.at[2 * side + 1 - x, :, b2], x2.at[side, :, h], xdev, x_in[k] + side)
+
+        return step
+
+    def stage_one(k):
+        def step():
+            both, a, b2, h, width = parts(k)
+            mine, new, y1, x1, x2, y2 = bufs(k)
+            for side in range(2):
+                net.wait(y1.at[side, :, h], y_in[k] + side)
+                add_into(mine.at[2 * y + side, :, a], y1.at[side, :, h], width)
+            net.send(mine.at[2 * y + 1 - x, :, a], x1.at[:, h], xdev, x_in[k] + 2)
+            for side in range(2):
+                net.wait(x2.at[side, :, h], x_in[k] + side)
+                add_into(mine.at[2 * side + x, :, b2], x2.at[side, :, h], width)
+            net.send(mine.at[2 * (1 - y) + x, :, b2], y2.at[:, h], ydev, y_in[k] + 2)
+
+        return step
+
+    def stage_two(k):
+        def step():
+            both, a, b2, h, width = parts(k)
+            mine, new, y1, x1, x2, y2 = bufs(k)
+            net.wait(x1.at[:, h], x_in[k] + 2)
+            add_into(mine.at[2 * y + x, :, a], x1.at[:, h], width)
+            net.wait(y2.at[:, h], y_in[k] + 2)
+            add_into(mine.at[2 * y + x, :, b2], y2.at[:, h], width)
+            if chunks[k][0] == "d":
+                for peer, pz in peers:
+                    net.send(
+                        pd.at[2 * y + x, rows_of(96 * pz, 96), both], rzd.at[z, :, both], peer, z_in[k] + z
+                    )
+                net.local(pd.at[2 * y + x, rows_of(96 * z, 96), both], rzd.at[z, :, both], z_in[k] + z)
+            else:
+                split_rows(pr.at[2 * y + x, :, both], sp.at[:, :, both], 384)
+                for peer, pz in peers:
+                    net.send(sp.at[pz, :, both], rz.at[z, :, both], peer, z_in[k] + z)
+                net.local(sp.at[z, :, both], rz.at[z, :, both], z_in[k] + z)
+
+        return step
+
+    def stage_sum(k):
+        def step():
+            both = parts(k)[0]
+            if chunks[k][0] == "d":
+                stage, total, width = rzd, sum_d, 256
+            else:
+                stage, total, width = rz, sum_r, 384
+            for part in range(4):
+                net.wait(stage.at[part, :, both], z_in[k] + part)
+            sum_parts(stage.at[:, :, both], total.at[:, both], width)
+
+        return step
+
+    pump = Pump()
+    for k in range(count + 3):
+        if k < count:
+            pump.add(stage_core(k))
+        if 0 <= k - 1 < count:
+            pump.add(stage_one(k - 1))
+        if 0 <= k - 2 < count:
+            pump.add(stage_two(k - 2))
+        if 0 <= k - 3 < count:
+            pump.add(stage_sum(k - 3))
+
+    got_mask, got_back = net.land(), net.land()
+    owner = device(y, lax.rem(z, 2), lax.div(z, 2), quarter)
+    is_owner = (lax.rem(z, 2) == x) & (lax.div(z, 2) == c) & (quarter == z)
+    net.send(masks, mask_rows, owner, got_mask, is_owner)
+    gz_in = net.land(4)
+    for peer, pz in peers:
+        net.send(gain_part, gz.at[z], peer, gz_in + z)
+    net.local(gain_part, gz.at[z], gz_in + z)
+    gh_in = net.land(3)
+
+    def gain_first():
+        for part in range(4):
+            net.wait(gz.at[part], gz_in + part)
+        gain_sum[...] = gz[0] + gz[1] + gz[2] + gz[3]
+        gh[0] = gain_sum[...]
+        net.send(gh.at[0], gh.at[3], xdev, gh_in)
+
+    def gain_next(i, to):
+        net.wait(gh.at[2 + i], gh_in + i - 1)
+        gain_sum[...] += gh[2 + i]
+        if to is not None:
+            gh[i] = gain_sum[...]
+            net.send(gh.at[i], gh.at[3 + i], to, gh_in + i)
+
+    lead_len, tail_len = aux[0:1, 0:1], aux[1:2, 0:1]
+    key_col = lax.broadcasted_iota(jnp.int32, (SLOT_ROWS, 1), 0)
+    key_seg, key_filler = segments(key_col, lead_len, tail_len)
+    key_seg = jnp.where(key_seg < 0, -5, key_seg)
+    masked = jnp.where(key_filler, -3e38, -1e30)
+    for head in range(3):
+        mine = own_lanes(c, head, (SLOT_ROWS, 256))
+        cols = pl.ds(256 * head, 256)
+        kh[:, cols] = jnp.where(mine, kr[...], 0.0).astype(BF)
+        vh[:, cols] = jnp.where(mine, vr[...], 0.0).astype(BF)
+    lane = lax.broadcasted_iota(jnp.int32, (8, 256), 1)
+    row8 = lax.broadcasted_iota(jnp.int32, (8, 256), 0)
+    picker = jnp.where((row8 < 3) & (lane // 64 - c == row8), 1.0, 0.0)
+    for n, q in enumerate([quarter] + [q for _, q in group]):
+        rows = rows_of(q * ROWS, ROWS)
+        net.wait(d_out.at[rows], got_do + q)
+        query, d_result = qr[rows, :], d_out[rows, :]
+        stat = stats[rows, :].T
+        product = d_result.astype(F32) * out[rows, :].astype(F32)
+        delta = lax.dot_general(
+            picker,
+            product,
+            (((1,), (1,)), ((), ())),
+            precision=lax.Precision.HIGHEST,
+            preferred_element_type=F32,
+        )
+        query_row = lax.broadcasted_iota(jnp.int32, (1, ROWS), 1) + q * ROWS
+        query_seg = segments(query_row, lead_len, tail_len)[0]
+        d_query = jnp.zeros((ROWS, 256), F32)
+        for head in range(3):
+            mine = own_lanes(c, head, (ROWS, 256))
+            cols = pl.ds(256 * head, 256)
+            key = kh[:, cols]
+            allowed = key_seg == query_seg
+            scores = jnp.where(allowed, nt(key, query), masked)
+            probs = jnp.exp(scores - stat[head : head + 1, :])
+            d_probs = nt(vh[:, cols], d_result)
+            d_scores = jnp.where(allowed, probs * (d_probs - delta[head : head + 1, :]), 0.0)
+            d_scores = d_scores.astype(BF)
+            d_query = d_query + tn(d_scores, key)
+            d_key = nn(d_scores, jnp.where(mine, query, 0.0).astype(BF))
+            d_value = nn(probs.astype(BF), jnp.where(mine, d_result, 0.0).astype(BF))
+            if n == 0 and head == 0:
+                dk[...] = d_key
+                dv[...] = d_value
+            else:
+                dk[...] += d_key
+                dv[...] += d_value
+            pump.run(2)
+            if n == 0 and head == 2:
+                gain_first()
+            if n > 0 and head == 2:
+                gain_next(n, (ydev, sib, None)[n - 1])
+        dqkv[rows, 0:256] = (d_query * 0.125).astype(BF)
+    dqkv[:, 256:512] = dk[...].astype(BF)
+    dqkv[:, 512:768] = dv[...].astype(BF)
+
+    fb_in, fc_in = net.land(2), net.land()
+    flip = quarter + 1 - 2 * c
+    cross = 2 - 4 * x
+
+    def first(q):
+        rows = rows_of(q * ROWS, ROWS)
+        d_first[rows, :] = nt(dqkv[rows, :], wp[...]).astype(BF)
+        return d_first.at[rows]
+
+    net.send(first(flip + cross), fb.at[0], sib, fb_in)
+    net.send(first(flip), fb.at[1], sib, fb_in + 1)
+    far = first(quarter + cross)
+    net.wait(fb.at[0], fb_in)
+    add_into(far, fb.at[0], 256)
+    net.send(far, fc, xdev, fc_in)
+    near = first(quarter)
+
+    qb_in = [net.land(4) for _ in range(3)]
+    qy_in, qx_in, qz_in = net.land(6), net.land(3), [net.land(4) for _ in range(3)]
+    first_core = c == 0
+
+    def q_make(part):
+        cols = pl.ds(256 * part, 256)
+        gq[:, cols] = tn(zn[...], dqkv[:, cols]).astype(BF)
+        for b in range(4):
+            net.send(gq.at[blk(tok_of(b, 1 - c)), cols], rq.at[b, :, cols], sib, qb_in[part] + b)
+
+    def q_core(part):
+        cols = pl.ds(256 * part, 256)
+        half = pl.ds(384 * part, 384)
+        base = 384 * part
+        for b in range(4):
+            net.wait(rq.at[b, :, cols], qb_in[part] + b)
+            own = gq[blk(tok_of(b, c)), cols].astype(F32)
+            new = rq[b, :, cols].astype(F32)
+            left, right = jnp.where(first_core, own, new), jnp.where(first_core, new, own)
+            hq[b, :, base : base + 128] = left[:, 0:128].astype(BF)
+            hq[b, :, base + 128 : base + 256] = (left[:, 128:256] + right[:, 0:128]).astype(BF)
+            hq[b, :, base + 256 : base + 384] = right[:, 128:256].astype(BF)
+        for side in range(2):
+            net.send(
+                hq.at[2 * (1 - y) + side, :, half], ryq.at[side, :, half], ydev, qy_in + 2 * part + side
+            )
+
+    def q_one(part):
+        half = pl.ds(384 * part, 384)
+        for side in range(2):
+            net.wait(ryq.at[side, :, half], qy_in + 2 * part + side)
+            add_into(hq.at[2 * y + side, :, half], ryq.at[side, :, half], 384)
+        net.send(hq.at[2 * y + 1 - x, :, half], rxq.at[:, half], xdev, qx_in + part)
+
+    def q_two(part):
+        half = pl.ds(384 * part, 384)
+        both = pl.ds(768 * part, 768)
+        net.wait(rxq.at[:, half], qx_in + part)
+        fq[:, lanes_of(768 * part + 384 * x, 384)] = hq[2 * y + x, :, half]
+        fq[:, lanes_of(768 * part + 384 * (1 - x), 384)] = rxq[:, half]
+        split_rows(fq.at[:, both], spq.at[:, :, both], 384)
+        for peer, pz in peers:
+            net.send(spq.at[pz, :, both], rzq.at[z, :, both], peer, qz_in[part] + z)
+        net.local(spq.at[z, :, both], rzq.at[z, :, both], qz_in[part] + z)
+
+    def q_sum(part):
+        both = pl.ds(768 * part, 768)
+        for src in range(4):
+            net.wait(rzq.at[src, :, both], qz_in[part] + src)
+        sum_parts(rzq.at[:, :, both], sum_q.at[:, both], 384)
+
+    q_make(0)
+    q_make(1)
+    q_core(0)
+    q_make(2)
+    q_core(1)
+    q_core(2)
+    net.wait(fb.at[1], fb_in + 1)
+    add_into(near, fb.at[1], 256)
+    q_one(0)
+    net.wait(fc, fc_in)
+    d_zn = near[...].astype(F32) + fc[...].astype(F32)
+    normed, scale = normalise(xb[...].astype(F32))
+    d_x = dh[...] + scale * (
+        d_zn
+        - jnp.mean(d_zn, axis=-1, keepdims=True)
+        - normed * jnp.mean(d_zn * normed, axis=-1, keepdims=True)
+    )
+    back[...] = d_x.astype(BF)
+    net.send(back, d_rows, owner, got_back, is_owner)
+    q_one(1)
+    q_two(0)
+    q_one(2)
+    q_two(1)
+    q_two(2)
+    pump.run()
+    for part in range(3):
+        q_sum(part)
+    net.wait(mask_rows, got_mask)
+    net.wait(d_rows, got_back)
+    net.finish()
+
+
+VMEM_SPEC = pl.BlockSpec(memory_space=pltpu.VMEM)
+ANY_SPEC = pl.BlockSpec(memory_space=pl.ANY)
+
+
+def call(body, ident, specs, outs, scratch, sems, args, cost):
+    out_shape = tuple(jax.ShapeDtypeStruct(shape, kind) for shape, kind, _ in outs)
+    scratch_shapes = [pltpu.VMEM(shape, kind) for shape, kind in scratch]
+    if sems:
+        scratch_shapes += [pltpu.SemaphoreType.DMA((n,)) for n in sems]
+    extra = {} if ident is None else dict(collective_id=ident, has_side_effects=True)
+    return pl.pallas_call(
+        body,
+        out_shape=out_shape,
+        in_specs=list(specs),
+        out_specs=tuple(spec for _, _, spec in outs),
+        scratch_shapes=scratch_shapes,
+        compiler_params=pltpu.CompilerParams(vmem_limit_bytes=63 * 2**20, **extra),
+        cost_estimate=pl.CostEstimate(flops=cost, bytes_accessed=2**24, transcendentals=0),
+    )(*args)
+
+
+def home_plan(
+    patches,
+    classes,
+    slot_lengths,
+    w_qkv,
+    w_out,
+    w_up,
+    w_down,
+    w_patch,
+    w_class,
+    norm1,
+    norm2,
+    mask_gain,
+    d_masks,
+):
+    V, A = VMEM_SPEC, ANY_SPEC
+    xin = jnp.concatenate([patches, jnp.pad(classes, ((0, CLS - REAL), (0, 0)))], axis=0)
+    pad_cols = ((0, 0), (0, 0), (0, CLS - REAL))
+    dmx = jnp.pad(d_masks.reshape(PATCH, 2, REAL), pad_cols).reshape(PATCH, 2 * CLS)
+    dmx = jnp.pad(dmx, ((0, 0), (0, 256 - 2 * CLS))).astype(BF)
+    gain = jnp.pad(mask_gain.reshape(1, 2, REAL), pad_cols).reshape(1, 2 * CLS)
+    gain = jnp.pad(gain, ((0, 7), (0, 256 - 2 * CLS)))
+    aux = jnp.broadcast_to(jnp.pad(slot_lengths.reshape(2, 1), ((0, 6), (0, 0))), (8, 128))
+    g1, g2 = norm1.astype(F32)[:, None], norm2.astype(F32)[:, None]
+    wqa = (w_qkv.astype(F32) * g1).astype(BF)
+    wra = jnp.concatenate([w_out, (w_up.astype(F32) * g2).astype(BF), w_patch, w_class], axis=1)
+    wide = wra.shape[1]
+    slot, part = (SLOT_ROWS, 768), (SLOT_ROWS, 256)
+    row_shape = (ROWS, 768)
+    (
+        gr, gd, dh, dob, masks, gain_part, zn, qr, kr, vr, out, stats, wp, xb, auxh
+    ) = call(
+        front_kernel,
+        1,
+        [V] * 7,
+        [
+            ((768, wide), BF, A),
+            ((3072, 768), BF, A),
+            (row_shape, F32, V),
+            (row_shape, BF, V),
+            ((PATCH, 256), BF, V),
+            ((8, 256), F32, V),
+            (slot, BF, A),
+            (part, BF, A),
+            (part, BF, A),
+            (part, BF, A),
+            (part, BF, A),
+            ((SLOT_ROWS, 128), F32, A),
+            ((768, 768), BF, A),
+            (row_shape, BF, A),
+            ((8, 128), jnp.int32, A),
+        ],
+        [
+            (slot, BF),
+            (slot, BF),
+            (part, BF),
+            (part, BF),
+            (part, BF),
+            (part, BF),
+            ((SLOT_ROWS, 128), F32),
+            ((768, 768), BF),
+            ((768, 1152), BF),
+            ((768, wide), BF),
+            ((3072, 768), BF),
+            ((4, 24, 2304), BF),
+            ((4, 24, wide), BF),
+            ((96, 2304), BF),
+            (slot, BF),
+            (slot, BF),
+            ((768, wide), BF),
+            ((3072, 768), BF),
+            ((PATCH, 256), BF),
+            ((8, 128), jnp.int32),
+            ((4, ROWS, 256), BF),
+            (row_shape, BF),
+            ((768, ROWS), BF),
+            (row_shape, BF),
+            (row_shape, F32),
+            (row_shape, F32),
+            (row_shape, BF),
+            ((PATCH, 768), F32),
+            ((4 * CLS, 768), BF),
+            ((4 * CLS, 768), BF),
+            ((4, CLS, 768), BF),
+            ((ROWS, 128), F32),
+        ],
+        (180, 240),
+        (xin, dmx, aux, wqa, wra, w_down, gain),
+        10**10,
+    )
+    half = wide // 2
+    d_rows, mask_rows, sum_q, sum_r, sum_d, gain_sum = call(
+        back_kernel,
+        2,
+        [A, A] + [V] * 11 + [A, V],
+        [
+            (row_shape, BF, A),
+            ((PATCH, 256), BF, A),
+            ((24, 2304), F32, V),
+            ((24, wide), F32, V),
+            ((96, 768), F32, V),
+            ((8, 256), F32, V),
+        ],
+        [
+            ((4, 96, wide), BF),
+            ((4, 384, 768), BF),
+            ((4, 96, wide), BF),
+            ((4, 384, 768), BF),
+            ((2, 96, half), BF),
+            ((96, half), BF),
+            ((2, 96, half), BF),
+            ((96, half), BF),
+            ((2, 384, 384), BF),
+            ((384, 384), BF),
+            ((2, 384, 384), BF),
+            ((384, 384), BF),
+            ((4, 24, wide), BF),
+            ((4, 24, wide), BF),
+            ((4, 96, 768), BF),
+            ((768, 768), BF),
+            ((4, 96, 768), BF),
+            ((4, 96, 1152), BF),
+            ((2, 96, 1152), BF),
+            ((96, 1152), BF),
+            ((96, 2304), BF),
+            ((4, 24, 2304), BF),
+            ((4, 24, 2304), BF),
+            (slot, BF),
+            ((2, ROWS, 768), BF),
+            (row_shape, BF),
+            (row_shape, BF),
+            ((4, 8, 256), F32),
+            ((6, 8, 256), F32),
+            (slot, BF),
+            (slot, BF),
+            (slot, BF),
+            (part, F32),
+            (part, F32),
+            (part, BF),
+        ],
+        (160, 220),
+        (gr, gd, zn, qr, kr, vr, out, stats, dob, wp, auxh, dh, xb, masks, gain_part),
+        10**10,
+    )
+
+    def unpad(values):
+        return values[:, 0 : 2 * CLS].reshape(-1, 2, CLS)[:, :, 0:REAL].reshape(-1, 2 * REAL)
+
+    d_rows = d_rows.astype(F32)
+    sum_up = sum_r[:, UP_AT : UP_AT + 3072]
+    return (
+        unpad(mask_rows).astype(F32),
+        d_rows[0:PATCH],
+        d_rows[PATCH : PATCH + REAL],
+        sum_q * g1,
+        sum_r[:, OUT_AT : OUT_AT + 768],
+        sum_up * g2,
+        sum_d,
+        sum_r[:, PATCH_AT : PATCH_AT + 768],
+        sum_r[:, CLASS_AT : CLASS_AT + 768],
+        jnp.sum(sum_q * w_qkv.astype(F32), axis=1),
+        jnp.sum(sum_up * w_up.astype(F32), axis=1),
+        unpad(gain_sum[0:1])[0],
+    )
+
+
 def solution(mesh):
     placed = (
         P(("tok", "head"), None),
@@ -269,8 +1405,9 @@
         P(),
         P(("tok", "head"), None),
     )
+    fits = mesh.shape["tok"] == 8 and mesh.shape["head"] == 4
     return jax.shard_map(
-        per_device,
+        home_plan if fits else per_device,
         mesh=mesh,
         in_specs=placed,
         out_specs=(

time: 1150 us -> 317 us (0.28)
  waiting for transfers between devices: 688 us -> 0 us
  Pallas kernels: 0 us -> 285 us
  blocking collectives: 178 us -> 0 us
  matrix products: 108 us -> 0 us
  local copies, waits for them, and re-layouts: 110 us -> 12.7 us
  between operations: 17.4 us -> 0.92 us
  starting transfers between devices: 15.7 us -> 0 us
  other arithmetic: 25.1 us -> 13 us
    reduce_scatter x6 -> x0, waiting for transfers between devices: 450 us -> none  [the longest x1 139 us: per_device(): lax.psum_scatter(flat_rows(grad_down_w), ('tok', 'head'), scatter_dimensi...]
    pallas_call x0 -> x2, Pallas kernels: none -> 285 us  [call(): pl.pallas_call(body, out_shape=out_shape, in_specs=list(specs), out_specs...]
    all_gather x6 -> x0, waiting for transfers between devices: 172 us -> none  [the longest x1 51.3 us: per_device(): lax.all_gather(shards[3], ('tok', 'head'), axis=0, tiled=True)]
    dot_general x42 -> x0, matrix products: 108 us -> none  [the longest x16 41.1 us: dot_right_t(): lax.dot_general(left, right, (((1,), (1,)), ((), ())), preferred_element_...]
    unnamed x3 -> x0, blocking collectives: 98.7 us -> none
    all_to_all x1 -> x0, blocking collectives: 64 us -> none  [per_device(): lax.all_to_all(d_moved, 'head', split_axis=0, concat_axis=2, tiled=True)]
    all_to_all x3 -> x0, waiting for transfers between devices: 63.4 us -> none  [the longest x1 39.5 us: per_device(): lax.all_to_all(qkv_rows, 'head', split_axis=2, concat_axis=0, tiled=True)]
    reshape x17 -> x5, local copies, waits for them, and re-layouts: 52.1 us -> 1.05 us  [the longest x2 0.84 us: home_plan(): gain = jnp.pad(mask_gain.reshape(1, 2, REAL), pad_cols).reshape(1, 2 * CLS)]
  transfers between devices with their start and end apart: 16 -> 0, of which waited for: 12 -> 0; matrix products, arithmetic and copies ran while one was open for 20% -> 0% of each run, Pallas kernels for 0% -> 0%
where the time goes in v2:
time: 317 us; the launch traced here: 311 us
  Pallas kernels  285 us (90%)
  other arithmetic  13 us (4%)
  local copies, waits for them, and re-layouts  12.7 us (4%)
    pallas_call x2, Pallas kernels, call(): pl.pallas_call(body, out_shape=out_shape, in_specs=list(specs), out_specs...  285 us

profile of v2, /device:TPU:0, one launch (start us, length us, event | category | flops | bytes accessed | tf_op | source)
XLA Modules:
  0.0 311.1 jit_solution(3269099726319857105)
XLA Ops:
  0.6 0.7 convert_element_type.41
  1.3 0.7 convert_element_type.44
  2.0 0.7 pad_bitcast_fusion
  2.6 0.8 reshape.55
  3.4 0.1 reshape.56
  3.5 0.7 broadcast_in_dim.10.aux_in
  4.1 0.6 pad.31.gain
  4.7 0.9 convert.9
  5.7 0.1 copy.27
  5.8 0.7 pad.28.dmx
  6.5 1.6 fusion.4.wqa
  8.1 1.0 fusion.2
  9.1 1.5 pad_maximum_fusion.wra
  10.6 1.9 fusion.1.xin
  12.5 158.9 %shard_map.220 = (bf16[768,5376]{1,0:T(8,128)(2,1)}, bf16[3072,768]{1,0:T(8,128)(2,1)}, f32[336,768]{1,0:T(8,128)}, bf16[336,768]{1,0:T(8,128)(2,1)}, bf16[256,2...) custom-call(bf16[336,768]{1,0:T(8,128)(2,1)} %fusion.1.xin, ...), custom_call_target="tpu_custom_call" | custom-call | flops 10000000000 | bytes 16777216 | tf_op jit(solution)/shard_map/pallas_call | solution.py:1215
  171.4 0.0 copy-start
  171.4 0.0 copy-start.1
  171.4 125.7 %shard_map.221 = (bf16[336,768]{1,0:T(8,128)(2,1)}, bf16[256,256]{1,0:T(8,128)(2,1)}, f32[24,2304]{1,0:T(8,128)}, f32[24,5376]{1,0:T(8,128)}, f32[96,768]{1,0:T(8,128)}, /*index=5*/f32[8,256]{1,0:T(8,128)}) custom-call(bf16[768,5376]{1,0:T(8,128)(2,1)} %get-tuple-element.33.gr, bf16[3072,768]{1,0:T(8,128)(2,1)} %get-tuple-element.34.gd, ...), custom_call_target="tpu_custom_call" | custom-call | flops 10000000000 | bytes 16777216 | tf_op jit(solution)/shard_map/pallas_call | solution.py:1215
  297.1 0.0 copy-start.2
  297.1 1.0 copy.28
  298.2 0.7 slice_reduce_fusion
  298.9 0.1 reshape.58
  299.0 0.6 squeeze_reshape.3
  299.6 0.7 reshape.59
  300.3 1.6 fusion.6
  302.0 0.0 copy-done
  302.0 2.4 fusion.3
  304.4 0.0 copy-done.1
  304.4 2.3 fusion.5
  306.7 1.6 slice.44
  308.3 1.9 slice.43
  310.2 0.7 copy.30
  (5 shorter events, 0.1 us)
Async XLA Ops:
  171.4 130.6 %copy-start = (bf16[24,3072]{1,0:T(8,128)(2,1)S(1)}, bf16[24,3072]{1,0:T(8,128)(2,1)}, u32[]{:S(2)}) copy-start(bf16[24,3072]{1,0:T(8,128)(2,1)} %param.18) | copy-start | bytes 442372
  171.4 133.0 %copy-start.1 = (bf16[24,2304]{1,0:T(8,128)(2,1)S(1)}, bf16[24,2304]{1,0:T(8,128)(2,1)}, u32[]{:S(2)}) copy-start(bf16[24,2304]{1,0:T(8,128)(2,1)} %param.16) | copy-start | bytes 331780
  297.1 13.1 %copy-start.2 = (f32[96,768]{1,0:T(8,128)S(1)}, f32[96,768]{1,0:T(8,128)}, u32[]{:S(2)}) copy-start(f32[96,768]{1,0:T(8,128)} %get-tuple-element.79) | copy-start | bytes 884740
